TPU v7x, 256 devices: a whole 4x4x8 slice. The times are simulated.
256 devices in a mesh: head: 8 (over y, x_hi), inner: 4 (over x_lo, core), outer: 8 (over z).
Axes of the slice: x: 4 (x_hi: 2, x_lo: 2; x = x_hi * 2 + x_lo), y: 4, z: 8, core: 2. Of those that a mesh axis runs over, the one named last changes fastest.
Arguments:
- queries: bfloat16 [16384, 4096], P(('head', 'inner', 'outer')), may hold values from -6 to 6
- key_rows: bfloat16 [16384, 1024], P(('head', 'inner', 'outer')), may hold values from -6 to 6
- value_rows: bfloat16 [16384, 1024], P(('head', 'inner', 'outer')), may hold values from -6 to 6
- outputs: bfloat16 [16384, 4096], P(('head', 'inner', 'outer')), may hold values from -1.5 to 1.5
- out_grads: bfloat16 [16384, 4096], P(('head', 'inner', 'outer')), may hold values from -24 to 24
- log_norms: float32 [32, 16384], P(None, ('head', 'inner', 'outer')), as said below
Outputs:
- query_grads: bfloat16 [16384, 4096], P(('head', 'inner', 'outer'))
- key_grads: bfloat16 [16384, 1024], P(('head', 'inner', 'outer'))
- value_grads: bfloat16 [16384, 1024], P(('head', 'inner', 'outer'))
Inputs may be any that keep to these rules, and one draw needn't show every extreme that they name: `log_norms`: within 1 of 0.5 * ln(p + 1) + 1.5, where p = (row index) % 2048 is the row's index in its sequence.
All inputs are finite; a program needn't handle non-finite values.
Results may differ from a plain program's by a relative error of at most 0.0051.
Values may be sent and summed in bfloat16 or wider, within the bound.
A program may use at most 128 MiB of HBM per device.

v0:
```python
import jax
import jax.numpy as jnp
from jax import lax
from jax.sharding import PartitionSpec as P

HQ = 32
HK = 8
HD = 128


def shifted(block, axis, distance):
    devices = range(lax.axis_size(axis))
    route = [((i - distance) % len(devices), i) for i in devices]
    return lax.ppermute(block, axis, route)


def global_positions(index, width, ctx_size):
    half = width // 2
    device = index // width
    within = index % width
    early = device * half + within
    late = (2 * ctx_size - 1 - device) * half + within - half
    return jnp.where(within < half, early, late)


def tile_grads(rows, k_part, v_part, k_pos, seq_count):
    q_part, do_part, lse_part, delta_part, q_pos = rows
    score_scale = HD ** (-0.5)
    kv_heads = k_part.shape[1] // HD
    group_size = HQ // HK
    q_count = q_part.shape[0] // seq_count
    k_count = k_part.shape[0] // seq_count
    q_heads = q_part.reshape(seq_count, q_count, kv_heads, group_size, HD)
    do_heads = do_part.reshape(seq_count, q_count, kv_heads, group_size, HD)
    k_heads = k_part.reshape(seq_count, k_count, kv_heads, HD)
    v_heads = v_part.reshape(seq_count, k_count, kv_heads, HD)
    scores = (
        jnp.einsum("stkgd,sukd->skgtu", q_heads, k_heads, preferred_element_type=jnp.float32)
        * score_scale
    )
    allowed = k_pos[None, :] <= q_pos[:, None]
    row_norms = jnp.transpose(
        lse_part.reshape(kv_heads, group_size, seq_count, q_count), (2, 0, 1, 3)
    )[..., None]
    weights = jnp.where(allowed, jnp.exp(scores - row_norms), 0.0)
    weights_low = weights.astype(jnp.bfloat16)
    dv_add = jnp.einsum(
        "skgtu,stkgd->sukd", weights_low, do_heads, preferred_element_type=jnp.float32
    )
    dweights = jnp.einsum(
        "stkgd,sukd->skgtu", do_heads, v_heads, preferred_element_type=jnp.float32
    )
    row_shift = jnp.transpose(
        delta_part.reshape(kv_heads, group_size, seq_count, q_count), (2, 0, 1, 3)
    )[..., None]
    dscores = (weights * (dweights - row_shift) * score_scale).astype(jnp.bfloat16)
    dq_add = jnp.einsum("skgtu,sukd->stkgd", dscores, k_heads, preferred_element_type=jnp.float32)
    dk_add = jnp.einsum("skgtu,stkgd->sukd", dscores, q_heads, preferred_element_type=jnp.float32)
    grad_add = jnp.stack(
        [dk_add.reshape(seq_count * k_count, -1), dv_add.reshape(seq_count * k_count, -1)]
    )
    return (dq_add.reshape(seq_count * q_count, -1), grad_add)


def block_grads(state, kv_pair, k_pos, seq_count):
    dq_add, grad_add = tile_grads(state, kv_pair[0], kv_pair[1], k_pos, seq_count)
    return (dq_add, grad_add)


def on_device(queries, key_rows, value_rows, outputs, out_grads, log_norms):
    seq_count = lax.axis_size("head")
    ctx_size = lax.axis_size(("inner", "outer"))
    width = queries.shape[0]
    q_all, k_all, v_all, out_all, do_all = (
        lax.all_to_all(queries, "head", split_axis=1, concat_axis=0, tiled=True),
        lax.all_to_all(key_rows, "head", split_axis=1, concat_axis=0, tiled=True),
        lax.all_to_all(value_rows, "head", split_axis=1, concat_axis=0, tiled=True),
        lax.all_to_all(outputs, "head", split_axis=1, concat_axis=0, tiled=True),
        lax.all_to_all(out_grads, "head", split_axis=1, concat_axis=0, tiled=True),
    )
    lse_all = lax.all_to_all(log_norms, "head", split_axis=0, concat_axis=1, tiled=True)
    rows_here = q_all.shape[0]
    product = do_all.reshape(rows_here, -1, HD).astype(jnp.float32) * out_all.reshape(
        rows_here, -1, HD
    ).astype(jnp.float32)
    delta_all = jnp.transpose(jnp.sum(product, axis=2))
    here = lax.axis_index(("inner", "outer"))
    q_pos = global_positions(here * width + jnp.arange(width, dtype=jnp.int32), width, ctx_size)
    state = (q_all, do_all, lse_all, delta_all, q_pos)
    kv_start = jnp.stack([k_all, v_all])
    grad_start = jnp.zeros(kv_start.shape, jnp.float32)
    dq_start = jnp.zeros(q_all.shape, jnp.float32)

    def cycle_step(turn, carry):
        kv_cur, grad_cur, dq_cur = carry
        anchor = (here - turn) % ctx_size
        k_pos = global_positions(
            anchor * width + jnp.arange(width, dtype=jnp.int32), width, ctx_size
        )
        dq_add, grad_add = block_grads(state, kv_cur, k_pos, seq_count)
        kv_next = shifted(kv_cur, ("inner", "outer"), 1)
        grad_next = shifted(grad_cur + grad_add, ("inner", "outer"), 1)
        return (kv_next, grad_next, dq_cur + dq_add)

    kv_end, grad_sum, dq_sum = lax.fori_loop(
        0, ctx_size, cycle_step, (kv_start, grad_start, dq_start)
    )
    grads_low = grad_sum.astype(jnp.bfloat16)
    query_grads, key_grads, value_grads = (
        lax.all_to_all(
            dq_sum.astype(jnp.bfloat16), "head", split_axis=0, concat_axis=1, tiled=True
        ),
        lax.all_to_all(grads_low[0], "head", split_axis=0, concat_axis=1, tiled=True),
        lax.all_to_all(grads_low[1], "head", split_axis=0, concat_axis=1, tiled=True),
    )
    return (query_grads, key_grads, value_grads)


def solution(mesh):
    placed = (
        P(("head", "inner", "outer"), None),
        P(("head", "inner", "outer"), None),
        P(("head", "inner", "outer"), None),
        P(("head", "inner", "outer"), None),
        P(("head", "inner", "outer"), None),
        P(None, ("head", "inner", "outer")),
    )
    return jax.shard_map(
        on_device,
        mesh=mesh,
        in_specs=placed,
        out_specs=(
            P(("head", "inner", "outer"), None),
            P(("head", "inner", "outer"), None),
            P(("head", "inner", "outer"), None),
        ),
        check_vma=False,
    )
```

profile of v0, /device:TPU:1, one launch (start us, length us, event | category | flops | bytes accessed | tf_op | source)
XLA Modules:
  0.0 894.3 jit_solution(9264947322814631845)
XLA Ops:
  81.1 779.5 %while.22 = (s32[]{:T(128)}, bf16[2,512,128]{2,1,0:T(8,128)(2,1)}, f32[2,512,128]{2,1,0:T(8,128)S(1)}, f32[512,512]{1,0:T(8,128)S(1)}, s32[]{:T(128)}, /*index=5...) while((s32[]{:T(128)}, bf16[2,512,128]{2,1,0:T(8,128)(2,1)}, ...), condition=%wide.wide.region_2.3_spmd.clone, body=%wide.wide.region_1.2_spmd.clone.sunk | while | flops 169614864 | bytes 18114008 | solution.py:105
  91.3 23.0 %collective-permute-done = bf16[2,512,128]{2,1,0:T(8,128)(2,1)} collective-permute-done((bf16[2,512,128]{2,1,0:T(8,128)(2,1)S(1)}, bf16[2,512,128]{2,1,0:T(8,128)(2,1)}, u32[]{:S(2)}, u32[]{:S(2)}) %collective-permute-start) | collective-permute-done | bytes 262176 | tf_op jit(solution)/shard_map/while/body/eval_jaxpr/ppermute | solution.py:14
  121.2 17.1 %collective-permute-done = bf16[2,512,128]{2,1,0:T(8,128)(2,1)} collective-permute-done((bf16[2,512,128]{2,1,0:T(8,128)(2,1)S(1)}, bf16[2,512,128]{2,1,0:T(8,128)(2,1)}, u32[]{:S(2)}, u32[]{:S(2)}) %collective-permute-start) | collective-permute-done | bytes 262176 | tf_op jit(solution)/shard_map/while/body/eval_jaxpr/ppermute | solution.py:14
  145.3 17.6 %collective-permute-done = bf16[2,512,128]{2,1,0:T(8,128)(2,1)} collective-permute-done((bf16[2,512,128]{2,1,0:T(8,128)(2,1)S(1)}, bf16[2,512,128]{2,1,0:T(8,128)(2,1)}, u32[]{:S(2)}, u32[]{:S(2)}) %collective-permute-start) | collective-permute-done | bytes 262176 | tf_op jit(solution)/shard_map/while/body/eval_jaxpr/ppermute | solution.py:14
  169.9 18.2 %collective-permute-done = bf16[2,512,128]{2,1,0:T(8,128)(2,1)} collective-permute-done((bf16[2,512,128]{2,1,0:T(8,128)(2,1)S(1)}, bf16[2,512,128]{2,1,0:T(8,128)(2,1)}, u32[]{:S(2)}, u32[]{:S(2)}) %collective-permute-start) | collective-permute-done | bytes 262176 | tf_op jit(solution)/shard_map/while/body/eval_jaxpr/ppermute | solution.py:14
  195.0 18.7 %collective-permute-done = bf16[2,512,128]{2,1,0:T(8,128)(2,1)} collective-permute-done((bf16[2,512,128]{2,1,0:T(8,128)(2,1)S(1)}, bf16[2,512,128]{2,1,0:T(8,128)(2,1)}, u32[]{:S(2)}, u32[]{:S(2)}) %collective-permute-start) | collective-permute-done | bytes 262176 | tf_op jit(solution)/shard_map/while/body/eval_jaxpr/ppermute | solution.py:14
  220.7 19.4 %collective-permute-done = bf16[2,512,128]{2,1,0:T(8,128)(2,1)} collective-permute-done((bf16[2,512,128]{2,1,0:T(8,128)(2,1)S(1)}, bf16[2,512,128]{2,1,0:T(8,128)(2,1)}, u32[]{:S(2)}, u32[]{:S(2)}) %collective-permute-start) | collective-permute-done | bytes 262176 | tf_op jit(solution)/shard_map/while/body/eval_jaxpr/ppermute | solution.py:14
  247.1 18.9 %collective-permute-done = bf16[2,512,128]{2,1,0:T(8,128)(2,1)} collective-permute-done((bf16[2,512,128]{2,1,0:T(8,128)(2,1)S(1)}, bf16[2,512,128]{2,1,0:T(8,128)(2,1)}, u32[]{:S(2)}, u32[]{:S(2)}) %collective-permute-start) | collective-permute-done | bytes 262176 | tf_op jit(solution)/shard_map/while/body/eval_jaxpr/ppermute | solution.py:14
  273.0 18.0 %collective-permute-done = bf16[2,512,128]{2,1,0:T(8,128)(2,1)} collective-permute-done((bf16[2,512,128]{2,1,0:T(8,128)(2,1)S(1)}, bf16[2,512,128]{2,1,0:T(8,128)(2,1)}, u32[]{:S(2)}, u32[]{:S(2)}) %collective-permute-start) | collective-permute-done | bytes 262176 | tf_op jit(solution)/shard_map/while/body/eval_jaxpr/ppermute | solution.py:14
  298.0 17.1 %collective-permute-done = bf16[2,512,128]{2,1,0:T(8,128)(2,1)} collective-permute-done((bf16[2,512,128]{2,1,0:T(8,128)(2,1)S(1)}, bf16[2,512,128]{2,1,0:T(8,128)(2,1)}, u32[]{:S(2)}, u32[]{:S(2)}) %collective-permute-start) | collective-permute-done | bytes 262176 | tf_op jit(solution)/shard_map/while/body/eval_jaxpr/ppermute | solution.py:14
  322.2 15.9 %collective-permute-done = bf16[2,512,128]{2,1,0:T(8,128)(2,1)} collective-permute-done((bf16[2,512,128]{2,1,0:T(8,128)(2,1)S(1)}, bf16[2,512,128]{2,1,0:T(8,128)(2,1)}, u32[]{:S(2)}, u32[]{:S(2)}) %collective-permute-start) | collective-permute-done | bytes 262176 | tf_op jit(solution)/shard_map/while/body/eval_jaxpr/ppermute | solution.py:14
  345.8 15.3 %collective-permute-done = bf16[2,512,128]{2,1,0:T(8,128)(2,1)} collective-permute-done((bf16[2,512,128]{2,1,0:T(8,128)(2,1)S(1)}, bf16[2,512,128]{2,1,0:T(8,128)(2,1)}, u32[]{:S(2)}, u32[]{:S(2)}) %collective-permute-start) | collective-permute-done | bytes 262176 | tf_op jit(solution)/shard_map/while/body/eval_jaxpr/ppermute | solution.py:14
  368.6 18.1 %collective-permute-done = bf16[2,512,128]{2,1,0:T(8,128)(2,1)} collective-permute-done((bf16[2,512,128]{2,1,0:T(8,128)(2,1)S(1)}, bf16[2,512,128]{2,1,0:T(8,128)(2,1)}, u32[]{:S(2)}, u32[]{:S(2)}) %collective-permute-start) | collective-permute-done | bytes 262176 | tf_op jit(solution)/shard_map/while/body/eval_jaxpr/ppermute | solution.py:14
  393.6 16.0 %collective-permute-done = bf16[2,512,128]{2,1,0:T(8,128)(2,1)} collective-permute-done((bf16[2,512,128]{2,1,0:T(8,128)(2,1)S(1)}, bf16[2,512,128]{2,1,0:T(8,128)(2,1)}, u32[]{:S(2)}, u32[]{:S(2)}) %collective-permute-start) | collective-permute-done | bytes 262176 | tf_op jit(solution)/shard_map/while/body/eval_jaxpr/ppermute | solution.py:14
  418.1 15.1 %collective-permute-done = bf16[2,512,128]{2,1,0:T(8,128)(2,1)} collective-permute-done((bf16[2,512,128]{2,1,0:T(8,128)(2,1)S(1)}, bf16[2,512,128]{2,1,0:T(8,128)(2,1)}, u32[]{:S(2)}, u32[]{:S(2)}) %collective-permute-start) | collective-permute-done | bytes 262176 | tf_op jit(solution)/shard_map/while/body/eval_jaxpr/ppermute | solution.py:14
  465.3 15.4 %collective-permute-done = bf16[2,512,128]{2,1,0:T(8,128)(2,1)} collective-permute-done((bf16[2,512,128]{2,1,0:T(8,128)(2,1)S(1)}, bf16[2,512,128]{2,1,0:T(8,128)(2,1)}, u32[]{:S(2)}, u32[]{:S(2)}) %collective-permute-start) | collective-permute-done | bytes 262176 | tf_op jit(solution)/shard_map/while/body/eval_jaxpr/ppermute | solution.py:14
  487.7 16.9 %collective-permute-done = bf16[2,512,128]{2,1,0:T(8,128)(2,1)} collective-permute-done((bf16[2,512,128]{2,1,0:T(8,128)(2,1)S(1)}, bf16[2,512,128]{2,1,0:T(8,128)(2,1)}, u32[]{:S(2)}, u32[]{:S(2)}) %collective-permute-start) | collective-permute-done | bytes 262176 | tf_op jit(solution)/shard_map/while/body/eval_jaxpr/ppermute | solution.py:14
  511.5 16.6 %collective-permute-done = bf16[2,512,128]{2,1,0:T(8,128)(2,1)} collective-permute-done((bf16[2,512,128]{2,1,0:T(8,128)(2,1)S(1)}, bf16[2,512,128]{2,1,0:T(8,128)(2,1)}, u32[]{:S(2)}, u32[]{:S(2)}) %collective-permute-start) | collective-permute-done | bytes 262176 | tf_op jit(solution)/shard_map/while/body/eval_jaxpr/ppermute | solution.py:14
  535.2 16.9 %collective-permute-done = bf16[2,512,128]{2,1,0:T(8,128)(2,1)} collective-permute-done((bf16[2,512,128]{2,1,0:T(8,128)(2,1)S(1)}, bf16[2,512,128]{2,1,0:T(8,128)(2,1)}, u32[]{:S(2)}, u32[]{:S(2)}) %collective-permute-start) | collective-permute-done | bytes 262176 | tf_op jit(solution)/shard_map/while/body/eval_jaxpr/ppermute | solution.py:14
  559.0 16.6 %collective-permute-done = bf16[2,512,128]{2,1,0:T(8,128)(2,1)} collective-permute-done((bf16[2,512,128]{2,1,0:T(8,128)(2,1)S(1)}, bf16[2,512,128]{2,1,0:T(8,128)(2,1)}, u32[]{:S(2)}, u32[]{:S(2)}) %collective-permute-start) | collective-permute-done | bytes 262176 | tf_op jit(solution)/shard_map/while/body/eval_jaxpr/ppermute | solution.py:14
  582.6 16.9 %collective-permute-done = bf16[2,512,128]{2,1,0:T(8,128)(2,1)} collective-permute-done((bf16[2,512,128]{2,1,0:T(8,128)(2,1)S(1)}, bf16[2,512,128]{2,1,0:T(8,128)(2,1)}, u32[]{:S(2)}, u32[]{:S(2)}) %collective-permute-start) | collective-permute-done | bytes 262176 | tf_op jit(solution)/shard_map/while/body/eval_jaxpr/ppermute | solution.py:14
  606.5 16.6 %collective-permute-done = bf16[2,512,128]{2,1,0:T(8,128)(2,1)} collective-permute-done((bf16[2,512,128]{2,1,0:T(8,128)(2,1)S(1)}, bf16[2,512,128]{2,1,0:T(8,128)(2,1)}, u32[]{:S(2)}, u32[]{:S(2)}) %collective-permute-start) | collective-permute-done | bytes 262176 | tf_op jit(solution)/shard_map/while/body/eval_jaxpr/ppermute | solution.py:14
  630.1 16.9 %collective-permute-done = bf16[2,512,128]{2,1,0:T(8,128)(2,1)} collective-permute-done((bf16[2,512,128]{2,1,0:T(8,128)(2,1)S(1)}, bf16[2,512,128]{2,1,0:T(8,128)(2,1)}, u32[]{:S(2)}, u32[]{:S(2)}) %collective-permute-start) | collective-permute-done | bytes 262176 | tf_op jit(solution)/shard_map/while/body/eval_jaxpr/ppermute | solution.py:14
  654.0 16.6 %collective-permute-done = bf16[2,512,128]{2,1,0:T(8,128)(2,1)} collective-permute-done((bf16[2,512,128]{2,1,0:T(8,128)(2,1)S(1)}, bf16[2,512,128]{2,1,0:T(8,128)(2,1)}, u32[]{:S(2)}, u32[]{:S(2)}) %collective-permute-start) | collective-permute-done | bytes 262176 | tf_op jit(solution)/shard_map/while/body/eval_jaxpr/ppermute | solution.py:14
  677.6 16.9 %collective-permute-done = bf16[2,512,128]{2,1,0:T(8,128)(2,1)} collective-permute-done((bf16[2,512,128]{2,1,0:T(8,128)(2,1)S(1)}, bf16[2,512,128]{2,1,0:T(8,128)(2,1)}, u32[]{:S(2)}, u32[]{:S(2)}) %collective-permute-start) | collective-permute-done | bytes 262176 | tf_op jit(solution)/shard_map/while/body/eval_jaxpr/ppermute | solution.py:14
  701.4 16.6 %collective-permute-done = bf16[2,512,128]{2,1,0:T(8,128)(2,1)} collective-permute-done((bf16[2,512,128]{2,1,0:T(8,128)(2,1)S(1)}, bf16[2,512,128]{2,1,0:T(8,128)(2,1)}, u32[]{:S(2)}, u32[]{:S(2)}) %collective-permute-start) | collective-permute-done | bytes 262176 | tf_op jit(solution)/shard_map/while/body/eval_jaxpr/ppermute | solution.py:14
  725.0 16.9 %collective-permute-done = bf16[2,512,128]{2,1,0:T(8,128)(2,1)} collective-permute-done((bf16[2,512,128]{2,1,0:T(8,128)(2,1)S(1)}, bf16[2,512,128]{2,1,0:T(8,128)(2,1)}, u32[]{:S(2)}, u32[]{:S(2)}) %collective-permute-start) | collective-permute-done | bytes 262176 | tf_op jit(solution)/shard_map/while/body/eval_jaxpr/ppermute | solution.py:14
  748.9 16.6 %collective-permute-done = bf16[2,512,128]{2,1,0:T(8,128)(2,1)} collective-permute-done((bf16[2,512,128]{2,1,0:T(8,128)(2,1)S(1)}, bf16[2,512,128]{2,1,0:T(8,128)(2,1)}, u32[]{:S(2)}, u32[]{:S(2)}) %collective-permute-start) | collective-permute-done | bytes 262176 | tf_op jit(solution)/shard_map/while/body/eval_jaxpr/ppermute | solution.py:14
  772.5 16.9 %collective-permute-done = bf16[2,512,128]{2,1,0:T(8,128)(2,1)} collective-permute-done((bf16[2,512,128]{2,1,0:T(8,128)(2,1)S(1)}, bf16[2,512,128]{2,1,0:T(8,128)(2,1)}, u32[]{:S(2)}, u32[]{:S(2)}) %collective-permute-start) | collective-permute-done | bytes 262176 | tf_op jit(solution)/shard_map/while/body/eval_jaxpr/ppermute | solution.py:14
  796.4 16.6 %collective-permute-done = bf16[2,512,128]{2,1,0:T(8,128)(2,1)} collective-permute-done((bf16[2,512,128]{2,1,0:T(8,128)(2,1)S(1)}, bf16[2,512,128]{2,1,0:T(8,128)(2,1)}, u32[]{:S(2)}, u32[]{:S(2)}) %collective-permute-start) | collective-permute-done | bytes 262176 | tf_op jit(solution)/shard_map/while/body/eval_jaxpr/ppermute | solution.py:14
  820.0 16.9 %collective-permute-done = bf16[2,512,128]{2,1,0:T(8,128)(2,1)} collective-permute-done((bf16[2,512,128]{2,1,0:T(8,128)(2,1)S(1)}, bf16[2,512,128]{2,1,0:T(8,128)(2,1)}, u32[]{:S(2)}, u32[]{:S(2)}) %collective-permute-start) | collective-permute-done | bytes 262176 | tf_op jit(solution)/shard_map/while/body/eval_jaxpr/ppermute | solution.py:14
  843.9 16.6 %collective-permute-done = bf16[2,512,128]{2,1,0:T(8,128)(2,1)} collective-permute-done((bf16[2,512,128]{2,1,0:T(8,128)(2,1)S(1)}, bf16[2,512,128]{2,1,0:T(8,128)(2,1)}, u32[]{:S(2)}, u32[]{:S(2)}) %collective-permute-start) | collective-permute-done | bytes 262176 | tf_op jit(solution)/shard_map/while/body/eval_jaxpr/ppermute | solution.py:14
  (890 shorter events, 358.2 us)
Async XLA Ops:
  85.8 28.5 %collective-permute-start.1 = (f32[2,512,128]{2,1,0:T(8,128)}, f32[2,512,128]{2,1,0:T(8,128)S(1)}, u32[]{:S(2)}, u32[]{:S(2)}) collective-permute-start(f32[2,512,128]{2,1,0:T(8,128)} %maximum_add_fusion.3), channel_id=1, source_target_pairs={{31,0},{0,1},{1,2},{2,3},{3,4},{4,5},{5,6},{6,7},{7,8},{8,9},{9,10... | collective-permute-start | bytes 1572872 | tf_op jit(solution)/shard_map/while/body/eval_jaxpr/ppermute | solution.py:14
  87.4 26.8 %collective-permute-start = (bf16[2,512,128]{2,1,0:T(8,128)(2,1)S(1)}, bf16[2,512,128]{2,1,0:T(8,128)(2,1)}, u32[]{:S(2)}, u32[]{:S(2)}) collective-permute-start(bf16[2,512,128]{2,1,0:T(8,128)(2,1)S(1)} %copy.140), channel_id=1, source_target_pairs={{31,0},{0,1},{1,2},{2,3},{3,4},{4,5},{5,6},{6,7},{7,8},{8,9},{9,10... | collective-permute-start | bytes 786440 | tf_op jit(solution)/shard_map/while/body/eval_jaxpr/ppermute | solution.py:14
  119.0 19.3 %collective-permute-start.1 = (f32[2,512,128]{2,1,0:T(8,128)}, f32[2,512,128]{2,1,0:T(8,128)S(1)}, u32[]{:S(2)}, u32[]{:S(2)}) collective-permute-start(f32[2,512,128]{2,1,0:T(8,128)} %maximum_add_fusion.3), channel_id=1, source_target_pairs={{31,0},{0,1},{1,2},{2,3},{3,4},{4,5},{5,6},{6,7},{7,8},{8,9},{9,10... | collective-permute-start | bytes 1572872 | tf_op jit(solution)/shard_map/while/body/eval_jaxpr/ppermute | solution.py:14
  119.0 19.3 %collective-permute-start = (bf16[2,512,128]{2,1,0:T(8,128)(2,1)S(1)}, bf16[2,512,128]{2,1,0:T(8,128)(2,1)}, u32[]{:S(2)}, u32[]{:S(2)}) collective-permute-start(bf16[2,512,128]{2,1,0:T(8,128)(2,1)S(1)} %copy.140), channel_id=1, source_target_pairs={{31,0},{0,1},{1,2},{2,3},{3,4},{4,5},{5,6},{6,7},{7,8},{8,9},{9,10... | collective-permute-start | bytes 786440 | tf_op jit(solution)/shard_map/while/body/eval_jaxpr/ppermute | solution.py:14
  143.1 19.9 %collective-permute-start.1 = (f32[2,512,128]{2,1,0:T(8,128)}, f32[2,512,128]{2,1,0:T(8,128)S(1)}, u32[]{:S(2)}, u32[]{:S(2)}) collective-permute-start(f32[2,512,128]{2,1,0:T(8,128)} %maximum_add_fusion.3), channel_id=1, source_target_pairs={{31,0},{0,1},{1,2},{2,3},{3,4},{4,5},{5,6},{6,7},{7,8},{8,9},{9,10... | collective-permute-start | bytes 1572872 | tf_op jit(solution)/shard_map/while/body/eval_jaxpr/ppermute | solution.py:14
  143.1 19.9 %collective-permute-start = (bf16[2,512,128]{2,1,0:T(8,128)(2,1)S(1)}, bf16[2,512,128]{2,1,0:T(8,128)(2,1)}, u32[]{:S(2)}, u32[]{:S(2)}) collective-permute-start(bf16[2,512,128]{2,1,0:T(8,128)(2,1)S(1)} %copy.140), channel_id=1, source_target_pairs={{31,0},{0,1},{1,2},{2,3},{3,4},{4,5},{5,6},{6,7},{7,8},{8,9},{9,10... | collective-permute-start | bytes 786440 | tf_op jit(solution)/shard_map/while/body/eval_jaxpr/ppermute | solution.py:14
  167.7 20.4 %collective-permute-start.1 = (f32[2,512,128]{2,1,0:T(8,128)}, f32[2,512,128]{2,1,0:T(8,128)S(1)}, u32[]{:S(2)}, u32[]{:S(2)}) collective-permute-start(f32[2,512,128]{2,1,0:T(8,128)} %maximum_add_fusion.3), channel_id=1, source_target_pairs={{31,0},{0,1},{1,2},{2,3},{3,4},{4,5},{5,6},{6,7},{7,8},{8,9},{9,10... | collective-permute-start | bytes 1572872 | tf_op jit(solution)/shard_map/while/body/eval_jaxpr/ppermute | solution.py:14
  167.7 20.4 %collective-permute-start = (bf16[2,512,128]{2,1,0:T(8,128)(2,1)S(1)}, bf16[2,512,128]{2,1,0:T(8,128)(2,1)}, u32[]{:S(2)}, u32[]{:S(2)}) collective-permute-start(bf16[2,512,128]{2,1,0:T(8,128)(2,1)S(1)} %copy.140), channel_id=1, source_target_pairs={{31,0},{0,1},{1,2},{2,3},{3,4},{4,5},{5,6},{6,7},{7,8},{8,9},{9,10... | collective-permute-start | bytes 786440 | tf_op jit(solution)/shard_map/while/body/eval_jaxpr/ppermute | solution.py:14
  192.8 21.0 %collective-permute-start.1 = (f32[2,512,128]{2,1,0:T(8,128)}, f32[2,512,128]{2,1,0:T(8,128)S(1)}, u32[]{:S(2)}, u32[]{:S(2)}) collective-permute-start(f32[2,512,128]{2,1,0:T(8,128)} %maximum_add_fusion.3), channel_id=1, source_target_pairs={{31,0},{0,1},{1,2},{2,3},{3,4},{4,5},{5,6},{6,7},{7,8},{8,9},{9,10... | collective-permute-start | bytes 1572872 | tf_op jit(solution)/shard_map/while/body/eval_jaxpr/ppermute | solution.py:14
  192.8 21.0 %collective-permute-start = (bf16[2,512,128]{2,1,0:T(8,128)(2,1)S(1)}, bf16[2,512,128]{2,1,0:T(8,128)(2,1)}, u32[]{:S(2)}, u32[]{:S(2)}) collective-permute-start(bf16[2,512,128]{2,1,0:T(8,128)(2,1)S(1)} %copy.140), channel_id=1, source_target_pairs={{31,0},{0,1},{1,2},{2,3},{3,4},{4,5},{5,6},{6,7},{7,8},{8,9},{9,10... | collective-permute-start | bytes 786440 | tf_op jit(solution)/shard_map/while/body/eval_jaxpr/ppermute | solution.py:14
  218.5 21.6 %collective-permute-start.1 = (f32[2,512,128]{2,1,0:T(8,128)}, f32[2,512,128]{2,1,0:T(8,128)S(1)}, u32[]{:S(2)}, u32[]{:S(2)}) collective-permute-start(f32[2,512,128]{2,1,0:T(8,128)} %maximum_add_fusion.3), channel_id=1, source_target_pairs={{31,0},{0,1},{1,2},{2,3},{3,4},{4,5},{5,6},{6,7},{7,8},{8,9},{9,10... | collective-permute-start | bytes 1572872 | tf_op jit(solution)/shard_map/while/body/eval_jaxpr/ppermute | solution.py:14
  218.5 21.6 %collective-permute-start = (bf16[2,512,128]{2,1,0:T(8,128)(2,1)S(1)}, bf16[2,512,128]{2,1,0:T(8,128)(2,1)}, u32[]{:S(2)}, u32[]{:S(2)}) collective-permute-start(bf16[2,512,128]{2,1,0:T(8,128)(2,1)S(1)} %copy.140), channel_id=1, source_target_pairs={{31,0},{0,1},{1,2},{2,3},{3,4},{4,5},{5,6},{6,7},{7,8},{8,9},{9,10... | collective-permute-start | bytes 786440 | tf_op jit(solution)/shard_map/while/body/eval_jaxpr/ppermute | solution.py:14
  244.9 21.2 %collective-permute-start.1 = (f32[2,512,128]{2,1,0:T(8,128)}, f32[2,512,128]{2,1,0:T(8,128)S(1)}, u32[]{:S(2)}, u32[]{:S(2)}) collective-permute-start(f32[2,512,128]{2,1,0:T(8,128)} %maximum_add_fusion.3), channel_id=1, source_target_pairs={{31,0},{0,1},{1,2},{2,3},{3,4},{4,5},{5,6},{6,7},{7,8},{8,9},{9,10... | collective-permute-start | bytes 1572872 | tf_op jit(solution)/shard_map/while/body/eval_jaxpr/ppermute | solution.py:14
  244.9 21.2 %collective-permute-start = (bf16[2,512,128]{2,1,0:T(8,128)(2,1)S(1)}, bf16[2,512,128]{2,1,0:T(8,128)(2,1)}, u32[]{:S(2)}, u32[]{:S(2)}) collective-permute-start(bf16[2,512,128]{2,1,0:T(8,128)(2,1)S(1)} %copy.140), channel_id=1, source_target_pairs={{31,0},{0,1},{1,2},{2,3},{3,4},{4,5},{5,6},{6,7},{7,8},{8,9},{9,10... | collective-permute-start | bytes 786440 | tf_op jit(solution)/shard_map/while/body/eval_jaxpr/ppermute | solution.py:14
  270.8 20.3 %collective-permute-start.1 = (f32[2,512,128]{2,1,0:T(8,128)}, f32[2,512,128]{2,1,0:T(8,128)S(1)}, u32[]{:S(2)}, u32[]{:S(2)}) collective-permute-start(f32[2,512,128]{2,1,0:T(8,128)} %maximum_add_fusion.3), channel_id=1, source_target_pairs={{31,0},{0,1},{1,2},{2,3},{3,4},{4,5},{5,6},{6,7},{7,8},{8,9},{9,10... | collective-permute-start | bytes 1572872 | tf_op jit(solution)/shard_map/while/body/eval_jaxpr/ppermute | solution.py:14
  270.8 20.3 %collective-permute-start = (bf16[2,512,128]{2,1,0:T(8,128)(2,1)S(1)}, bf16[2,512,128]{2,1,0:T(8,128)(2,1)}, u32[]{:S(2)}, u32[]{:S(2)}) collective-permute-start(bf16[2,512,128]{2,1,0:T(8,128)(2,1)S(1)} %copy.140), channel_id=1, source_target_pairs={{31,0},{0,1},{1,2},{2,3},{3,4},{4,5},{5,6},{6,7},{7,8},{8,9},{9,10... | collective-permute-start | bytes 786440 | tf_op jit(solution)/shard_map/while/body/eval_jaxpr/ppermute | solution.py:14
  295.8 19.3 %collective-permute-start.1 = (f32[2,512,128]{2,1,0:T(8,128)}, f32[2,512,128]{2,1,0:T(8,128)S(1)}, u32[]{:S(2)}, u32[]{:S(2)}) collective-permute-start(f32[2,512,128]{2,1,0:T(8,128)} %maximum_add_fusion.3), channel_id=1, source_target_pairs={{31,0},{0,1},{1,2},{2,3},{3,4},{4,5},{5,6},{6,7},{7,8},{8,9},{9,10... | collective-permute-start | bytes 1572872 | tf_op jit(solution)/shard_map/while/body/eval_jaxpr/ppermute | solution.py:14
  295.8 19.3 %collective-permute-start = (bf16[2,512,128]{2,1,0:T(8,128)(2,1)S(1)}, bf16[2,512,128]{2,1,0:T(8,128)(2,1)}, u32[]{:S(2)}, u32[]{:S(2)}) collective-permute-start(bf16[2,512,128]{2,1,0:T(8,128)(2,1)S(1)} %copy.140), channel_id=1, source_target_pairs={{31,0},{0,1},{1,2},{2,3},{3,4},{4,5},{5,6},{6,7},{7,8},{8,9},{9,10... | collective-permute-start | bytes 786440 | tf_op jit(solution)/shard_map/while/body/eval_jaxpr/ppermute | solution.py:14
  365.8 20.8 %collective-permute-start.1 = (f32[2,512,128]{2,1,0:T(8,128)}, f32[2,512,128]{2,1,0:T(8,128)S(1)}, u32[]{:S(2)}, u32[]{:S(2)}) collective-permute-start(f32[2,512,128]{2,1,0:T(8,128)} %maximum_add_fusion.3), channel_id=1, source_target_pairs={{31,0},{0,1},{1,2},{2,3},{3,4},{4,5},{5,6},{6,7},{7,8},{8,9},{9,10... | collective-permute-start | bytes 1572872 | tf_op jit(solution)/shard_map/while/body/eval_jaxpr/ppermute | solution.py:14
  365.8 20.8 %collective-permute-start = (bf16[2,512,128]{2,1,0:T(8,128)(2,1)S(1)}, bf16[2,512,128]{2,1,0:T(8,128)(2,1)}, u32[]{:S(2)}, u32[]{:S(2)}) collective-permute-start(bf16[2,512,128]{2,1,0:T(8,128)(2,1)S(1)} %copy.140), channel_id=1, source_target_pairs={{31,0},{0,1},{1,2},{2,3},{3,4},{4,5},{5,6},{6,7},{7,8},{8,9},{9,10... | collective-permute-start | bytes 786440 | tf_op jit(solution)/shard_map/while/body/eval_jaxpr/ppermute | solution.py:14
  438.0 19.1 %collective-permute-start.1 = (f32[2,512,128]{2,1,0:T(8,128)}, f32[2,512,128]{2,1,0:T(8,128)S(1)}, u32[]{:S(2)}, u32[]{:S(2)}) collective-permute-start(f32[2,512,128]{2,1,0:T(8,128)} %maximum_add_fusion.3), channel_id=1, source_target_pairs={{31,0},{0,1},{1,2},{2,3},{3,4},{4,5},{5,6},{6,7},{7,8},{8,9},{9,10... | collective-permute-start | bytes 1572872 | tf_op jit(solution)/shard_map/while/body/eval_jaxpr/ppermute | solution.py:14
  485.4 19.1 %collective-permute-start.1 = (f32[2,512,128]{2,1,0:T(8,128)}, f32[2,512,128]{2,1,0:T(8,128)S(1)}, u32[]{:S(2)}, u32[]{:S(2)}) collective-permute-start(f32[2,512,128]{2,1,0:T(8,128)} %maximum_add_fusion.3), channel_id=1, source_target_pairs={{31,0},{0,1},{1,2},{2,3},{3,4},{4,5},{5,6},{6,7},{7,8},{8,9},{9,10... | collective-permute-start | bytes 1572872 | tf_op jit(solution)/shard_map/while/body/eval_jaxpr/ppermute | solution.py:14
  485.4 19.1 %collective-permute-start = (bf16[2,512,128]{2,1,0:T(8,128)(2,1)S(1)}, bf16[2,512,128]{2,1,0:T(8,128)(2,1)}, u32[]{:S(2)}, u32[]{:S(2)}) collective-permute-start(bf16[2,512,128]{2,1,0:T(8,128)(2,1)S(1)} %copy.140), channel_id=1, source_target_pairs={{31,0},{0,1},{1,2},{2,3},{3,4},{4,5},{5,6},{6,7},{7,8},{8,9},{9,10... | collective-permute-start | bytes 786440 | tf_op jit(solution)/shard_map/while/body/eval_jaxpr/ppermute | solution.py:14
  532.9 19.1 %collective-permute-start.1 = (f32[2,512,128]{2,1,0:T(8,128)}, f32[2,512,128]{2,1,0:T(8,128)S(1)}, u32[]{:S(2)}, u32[]{:S(2)}) collective-permute-start(f32[2,512,128]{2,1,0:T(8,128)} %maximum_add_fusion.3), channel_id=1, source_target_pairs={{31,0},{0,1},{1,2},{2,3},{3,4},{4,5},{5,6},{6,7},{7,8},{8,9},{9,10... | collective-permute-start | bytes 1572872 | tf_op jit(solution)/shard_map/while/body/eval_jaxpr/ppermute | solution.py:14
  580.4 19.1 %collective-permute-start.1 = (f32[2,512,128]{2,1,0:T(8,128)}, f32[2,512,128]{2,1,0:T(8,128)S(1)}, u32[]{:S(2)}, u32[]{:S(2)}) collective-permute-start(f32[2,512,128]{2,1,0:T(8,128)} %maximum_add_fusion.3), channel_id=1, source_target_pairs={{31,0},{0,1},{1,2},{2,3},{3,4},{4,5},{5,6},{6,7},{7,8},{8,9},{9,10... | collective-permute-start | bytes 1572872 | tf_op jit(solution)/shard_map/while/body/eval_jaxpr/ppermute | solution.py:14
  580.4 19.1 %collective-permute-start = (bf16[2,512,128]{2,1,0:T(8,128)(2,1)S(1)}, bf16[2,512,128]{2,1,0:T(8,128)(2,1)}, u32[]{:S(2)}, u32[]{:S(2)}) collective-permute-start(bf16[2,512,128]{2,1,0:T(8,128)(2,1)S(1)} %copy.140), channel_id=1, source_target_pairs={{31,0},{0,1},{1,2},{2,3},{3,4},{4,5},{5,6},{6,7},{7,8},{8,9},{9,10... | collective-permute-start | bytes 786440 | tf_op jit(solution)/shard_map/while/body/eval_jaxpr/ppermute | solution.py:14
  627.9 19.1 %collective-permute-start.1 = (f32[2,512,128]{2,1,0:T(8,128)}, f32[2,512,128]{2,1,0:T(8,128)S(1)}, u32[]{:S(2)}, u32[]{:S(2)}) collective-permute-start(f32[2,512,128]{2,1,0:T(8,128)} %maximum_add_fusion.3), channel_id=1, source_target_pairs={{31,0},{0,1},{1,2},{2,3},{3,4},{4,5},{5,6},{6,7},{7,8},{8,9},{9,10... | collective-permute-start | bytes 1572872 | tf_op jit(solution)/shard_map/while/body/eval_jaxpr/ppermute | solution.py:14
  675.3 19.1 %collective-permute-start.1 = (f32[2,512,128]{2,1,0:T(8,128)}, f32[2,512,128]{2,1,0:T(8,128)S(1)}, u32[]{:S(2)}, u32[]{:S(2)}) collective-permute-start(f32[2,512,128]{2,1,0:T(8,128)} %maximum_add_fusion.3), channel_id=1, source_target_pairs={{31,0},{0,1},{1,2},{2,3},{3,4},{4,5},{5,6},{6,7},{7,8},{8,9},{9,10... | collective-permute-start | bytes 1572872 | tf_op jit(solution)/shard_map/while/body/eval_jaxpr/ppermute | solution.py:14
  722.8 19.1 %collective-permute-start.1 = (f32[2,512,128]{2,1,0:T(8,128)}, f32[2,512,128]{2,1,0:T(8,128)S(1)}, u32[]{:S(2)}, u32[]{:S(2)}) collective-permute-start(f32[2,512,128]{2,1,0:T(8,128)} %maximum_add_fusion.3), channel_id=1, source_target_pairs={{31,0},{0,1},{1,2},{2,3},{3,4},{4,5},{5,6},{6,7},{7,8},{8,9},{9,10... | collective-permute-start | bytes 1572872 | tf_op jit(solution)/shard_map/while/body/eval_jaxpr/ppermute | solution.py:14
  722.8 19.1 %collective-permute-start = (bf16[2,512,128]{2,1,0:T(8,128)(2,1)S(1)}, bf16[2,512,128]{2,1,0:T(8,128)(2,1)}, u32[]{:S(2)}, u32[]{:S(2)}) collective-permute-start(bf16[2,512,128]{2,1,0:T(8,128)(2,1)S(1)} %copy.140), channel_id=1, source_target_pairs={{31,0},{0,1},{1,2},{2,3},{3,4},{4,5},{5,6},{6,7},{7,8},{8,9},{9,10... | collective-permute-start | bytes 786440 | tf_op jit(solution)/shard_map/while/body/eval_jaxpr/ppermute | solution.py:14
  770.3 19.1 %collective-permute-start.1 = (f32[2,512,128]{2,1,0:T(8,128)}, f32[2,512,128]{2,1,0:T(8,128)S(1)}, u32[]{:S(2)}, u32[]{:S(2)}) collective-permute-start(f32[2,512,128]{2,1,0:T(8,128)} %maximum_add_fusion.3), channel_id=1, source_target_pairs={{31,0},{0,1},{1,2},{2,3},{3,4},{4,5},{5,6},{6,7},{7,8},{8,9},{9,10... | collective-permute-start | bytes 1572872 | tf_op jit(solution)/shard_map/while/body/eval_jaxpr/ppermute | solution.py:14
  817.8 19.1 %collective-permute-start.1 = (f32[2,512,128]{2,1,0:T(8,128)}, f32[2,512,128]{2,1,0:T(8,128)S(1)}, u32[]{:S(2)}, u32[]{:S(2)}) collective-permute-start(f32[2,512,128]{2,1,0:T(8,128)} %maximum_add_fusion.3), channel_id=1, source_target_pairs={{31,0},{0,1},{1,2},{2,3},{3,4},{4,5},{5,6},{6,7},{7,8},{8,9},{9,10... | collective-permute-start | bytes 1572872 | tf_op jit(solution)/shard_map/while/body/eval_jaxpr/ppermute | solution.py:14
  (143 other events, 1376.3 us)
where the time goes:
time: 905 us; the launch traced here: 894 us
  waiting for transfers between devices  602 us (67%)
  matrix products  98.5 us (11%)
  local copies, waits for them, and re-layouts  93.6 us (10%)
  other arithmetic  45.2 us (5%)
  starting transfers between devices  41.6 us (5%)
  blocking collectives  9.43 us (1%)
    ppermute x64, waiting for transfers between devices, shifted(): return lax.ppermute(block, axis, route)  547 us
    dot_general x32, matrix products, tile_grads(): jnp.einsum('skgtu,sukd->stkgd', dscores, k_heads, preferred_element_type=...  39.8 us
    while x224, local copies, waits for them, and re-layouts  30.9 us
    add x32, other arithmetic, cycle_step(): grad_next = shifted(grad_cur + grad_add, ('inner', 'outer'), 1)  27.5 us
    reshape x64, local copies, waits for them, and re-layouts, tile_grads(): delta_part.reshape(kv_heads, group_size, seq_count, q_count)  25.1 us
    transpose x32, local copies, waits for them, and re-layouts, tile_grads(): jnp.einsum('skgtu,sukd->stkgd', dscores, k_heads, preferred_element_type=...  21.8 us
    dot_general x32, matrix products, tile_grads(): jnp.einsum('stkgd,sukd->skgtu', q_heads, k_heads, preferred_element_type=...  20.6 us
    dot_general x32, matrix products, tile_grads(): jnp.einsum('stkgd,sukd->skgtu', do_heads, v_heads, preferred_element_type...  20.1 us
  transfers between devices with their start and end apart: 72, of which 40 were waited for; matrix products, arithmetic and copies ran while one was open for 9% of the time, Pallas kernels for 0%

commit v1 on v0

v1 whole, which is shorter than its diff:
```python
import functools

import jax
import jax.numpy as jnp
from jax import lax
from jax.experimental import pallas as pl
from jax.experimental.pallas import tpu as pltpu
from jax.sharding import PartitionSpec as P

HQ = 32
HK = 8
HD = 128
GROUP = HQ // HK
TOK = 64
HALF = TOK // 2
NZ = 8
NI = 4
GCOLS = GROUP * HD
LOG2E = 1.4426950408889634
SCALE = HD ** -0.5
MESH = pl.DeviceIdType.MESH
F32 = jnp.float32
BF16 = jnp.bfloat16
ORDER = (1, 7, 2, 6, 3, 5, 4)
GROUPS = ((0, 1), (7, 2), (6, 3), (5, 4))


def dot(a, b, dims):
    return lax.dot_general(a, b, (dims, ((), ())), preferred_element_type=F32)


def kernel(
    q_hbm, k_hbm, v_hbm, o_hbm, do_hbm, lse_hbm,
    dq_out, dk_out, dv_out,
    o_in, do_in, lse_in, lse_wide, aux_send, aux, kv, qb, dob,
    k_t, q_rows, do_rows, dq_acc, dq_stage, dk_acc, dv_acc,
    part_send, part_recv, kv_stage,
    local_sem, kv_s, kv_r, aux_s, aux_r, q_s, q_r, do_s, do_r,
    relay_s, relay_r, dq_s, dq_r, part_s, part_r, out_s, out_r,
):
    me = lax.axis_index("inner")
    z = lax.axis_index("outer")

    def ring(step):
        return lax.rem(z + step, NZ)

    def at_ring(step):
        return {"outer": ring(step)}

    def at_plane(x):
        return {"inner": me ^ x}

    def q_cols(index):
        return pl.ds(pl.multiple_of(index * GCOLS, GCOLS), GCOLS)

    def k_cols(index):
        return pl.ds(pl.multiple_of(index * HD, HD), HD)

    barrier = pltpu.get_barrier_semaphore()
    for step in range(1, NZ):
        pl.semaphore_signal(barrier, inc=1, device_id=at_ring(step), device_id_type=MESH)
    for x in range(1, NI):
        pl.semaphore_signal(barrier, inc=1, device_id=at_plane(x), device_id_type=MESH)

    locals_ = [
        pltpu.make_async_copy(k_hbm.at[:, k_cols(z)], kv.at[me, 0, 0], local_sem.at[0]),
        pltpu.make_async_copy(v_hbm.at[:, k_cols(z)], kv.at[me, 0, 1], local_sem.at[1]),
        pltpu.make_async_copy(q_hbm.at[:, q_cols(z)], qb.at[0], local_sem.at[2]),
        pltpu.make_async_copy(do_hbm.at[:, q_cols(z)], dob.at[0], local_sem.at[3]),
        pltpu.make_async_copy(o_hbm, o_in, local_sem.at[4]),
        pltpu.make_async_copy(do_hbm, do_in, local_sem.at[5]),
        pltpu.make_async_copy(lse_hbm, lse_in, local_sem.at[6]),
    ]
    for copy in locals_:
        copy.start()
    pl.semaphore_wait(barrier, NZ - 1 + NI - 1)

    def remote(src, dst, send, recv, where):
        return pltpu.make_async_remote_copy(
            src_ref=src, dst_ref=dst, send_sem=send, recv_sem=recv,
            device_id=where, device_id_type=MESH,
        )

    sends = []
    k_in = {}
    q_in = {}
    for step in ORDER:
        slot = NZ - step
        there = ring(step)
        pair = [
            remote(ref.at[:, k_cols(there)], kv.at[me, slot, n], kv_s.at[n, slot],
                   kv_r.at[n, slot], at_ring(step))
            for n, ref in enumerate((k_hbm, v_hbm))
        ]
        for copy in pair:
            copy.start()
        sends += pair
        k_in[slot] = pair

    for n in (4, 5, 6):
        locals_[n].wait()
    lse_wide[...] = jnp.zeros_like(lse_wide)
    lse_wide[:, 0:TOK] = lse_in[...]
    norms = lse_wide[...] * LOG2E
    rows = lax.broadcasted_iota(jnp.int32, norms.shape, 0)
    lanes = lax.broadcasted_iota(jnp.int32, norms.shape, 1)
    for late in range(2):
        picked = jnp.zeros_like(norms)
        for h in range(GROUP):
            moved = norms
            shift = (h - late) * HALF % HD
            if shift:
                moved = pltpu.roll(norms, shift, 1)
            here = (rows % GROUP == h) & (lanes // HALF == h)
            picked = jnp.where(here, moved, picked)
        total = picked
        for h in range(1, GROUP):
            total = total + pltpu.roll(picked, HQ - h, 0)
        for g in range(HK):
            aux_send[g, late:late + 1, :] = total[GROUP * g:GROUP * g + 1, :]
    ones = jnp.ones((8, HD), BF16)
    for g in range(HK):
        blocks = []
        for late in range(2):
            for h in range(GROUP):
                part = (slice(late * HALF, (late + 1) * HALF),
                        slice((g * GROUP + h) * HD, (g * GROUP + h + 1) * HD))
                blocks.append(do_in[part].astype(F32) * o_in[part].astype(F32))
        product = jnp.concatenate(blocks, axis=0)
        high = product.astype(BF16)
        low = (product - high.astype(F32)).astype(BF16)
        sums = dot(ones, high, ((1,), (1,))) + dot(ones, low, ((1,), (1,)))
        aux_send[g, 2:3, :] = sums[0:1, 0:HD]
        aux_send[g, 3:4, :] = sums[0:1, HD:2 * HD]
    aux[0] = aux_send[z]

    for step in ORDER:
        slot = NZ - step
        there = ring(step)
        trio = [
            remote(aux_send.at[there], aux.at[slot], aux_s.at[slot], aux_r.at[slot], at_ring(step)),
            remote(q_hbm.at[:, q_cols(there)], qb.at[slot], q_s.at[slot], q_r.at[slot], at_ring(step)),
            remote(do_hbm.at[:, q_cols(there)], dob.at[slot], do_s.at[slot], do_r.at[slot], at_ring(step)),
        ]
        for copy in trio:
            copy.start()
        sends += trio
        q_in[slot] = trio

    relays = {}
    for slot in (0,) + tuple(NZ - step for step in ORDER):
        if slot == 0:
            locals_[0].wait()
            locals_[1].wait()
        else:
            for copy in k_in[slot]:
                copy.wait_recv()
        for x in (3, 2, 1):
            copy = remote(kv.at[me, slot], kv.at[me, slot], relay_s.at[x - 1, slot],
                          relay_r.at[x - 1, slot], at_plane(x))
            copy.start()
            sends.append(copy)
            relays[x, slot] = copy

    def transpose_keys(owner):
        for late in range(2):
            rows_ = kv[owner, :, 0, late * HALF:(late + 1) * HALF, :].reshape(NZ * HALF, HD)
            k_t[late, owner] = rows_.T

    transpose_keys(me)
    for x in (1, 2, 3):
        for slot in range(NZ):
            pltpu.make_async_remote_copy(
                src_ref=kv.at[me ^ x, slot], dst_ref=kv.at[me ^ x, slot],
                send_sem=relay_s.at[x - 1, slot], recv_sem=relay_r.at[x - 1, slot],
                device_id=at_plane(x), device_id_type=MESH,
            ).wait_recv()
        transpose_keys(me ^ x)

    dk_acc[...] = jnp.zeros_like(dk_acc)
    dv_acc[...] = jnp.zeros_like(dv_acc)
    dq_sends = []

    for turn, slots in enumerate(GROUPS):
        last = turn == len(GROUPS) - 1
        width = len(slots) * GROUP * HALF
        for n, slot in enumerate(slots):
            if slot == 0:
                locals_[2].wait()
                locals_[3].wait()
            else:
                for copy in q_in[slot]:
                    copy.wait_recv()
            for late in range(2):
                for h in range(GROUP):
                    to = slice((n * GROUP + h) * HALF, (n * GROUP + h + 1) * HALF)
                    tok = slice(late * HALF, (late + 1) * HALF)
                    col = slice(h * HD, (h + 1) * HD)
                    q_rows[late, to, :] = qb[slot, tok, col]
                    do_rows[late, to, :] = dob[slot, tok, col]
        dq_acc[...] = jnp.zeros_like(dq_acc)

        def tile(q_late, k_late, owner, diagonal):
            tok = pl.ds(pl.multiple_of(k_late * HALF, HALF), HALF)
            keys = kv[owner, :, 0, tok, :].reshape(NZ * HALF, HD)
            values = kv[owner, :, 1, tok, :].reshape(NZ * HALF, HD)
            q_part = q_rows[q_late, 0:width]
            do_part = do_rows[q_late, 0:width]
            norm = jnp.concatenate([aux[slot, pl.ds(q_late, 1), :] for slot in slots], axis=1)
            delta = jnp.concatenate([aux[slot, pl.ds(q_late + 2, 1), :] for slot in slots], axis=1)
            scores = dot(keys, q_part, ((1,), (1,)))
            weights = jnp.exp2(scores * (SCALE * LOG2E) - norm)
            if diagonal:
                key_row = lax.broadcasted_iota(jnp.int32, (NZ * HALF, 1), 0)
                q_lane = lax.broadcasted_iota(jnp.int32, (1, width), 1)
                key_z = (z + key_row // HALF) % NZ
                q_slot = jnp.full((1, width), slots[0], jnp.int32)
                for n, slot in enumerate(slots):
                    q_slot = jnp.where(q_lane // (GROUP * HALF) == n, slot, q_slot)
                q_z = (z + q_slot) % NZ
                sign = 1 if diagonal == 1 else -1
                key_at = sign * key_z * HALF + key_row % HALF
                q_at = sign * q_z * HALF + q_lane % HALF
                weights = jnp.where(key_at <= q_at, weights, 0.0)
            weights_low = weights.astype(BF16)
            dv_acc[owner, :, tok, :] += dot(weights_low, do_part, ((1,), (0,))).reshape(NZ, HALF, HD)
            dweights = dot(values, do_part, ((1,), (1,)))
            dscores = (weights * (dweights - delta)).astype(BF16)
            dk_acc[owner, :, tok, :] += dot(dscores, q_part, ((1,), (0,))).reshape(NZ, HALF, HD)
            dq_acc[q_late, :, 0:width] += dot(k_t[k_late, owner], dscores, ((1,), (0,)))

        for x in (3, 2, 1):
            owner = me ^ x
            tile(1, 0, owner, 0)
            above = (owner > me).astype(jnp.int32)
            tile(above, above, owner, 0)
            if last:
                part_send[x - 1, :, 0] = dk_acc[owner].astype(BF16)
                part_send[x - 1, :, 1] = dv_acc[owner].astype(BF16)
                copy = remote(part_send.at[x - 1], part_recv.at[x - 1], part_s.at[x - 1],
                              part_r.at[x - 1], at_plane(x))
                copy.start()
                sends.append(copy)
                relays["part", x] = copy
        tile(1, 0, me, 0)
        tile(0, 0, me, 1)
        tile(1, 1, me, 2)

        for late in range(2):
            back = (dq_acc[late, :, 0:width] * SCALE).T.astype(BF16)
            for n, slot in enumerate(slots):
                for h in range(GROUP):
                    rows_ = slice((n * GROUP + h) * HALF, (n * GROUP + h + 1) * HALF)
                    dq_stage[slot, late * HALF:(late + 1) * HALF, h * HD:(h + 1) * HD] = back[rows_]
        for slot in slots:
            if slot == 0:
                copy = pltpu.make_async_copy(dq_stage.at[0], dq_out.at[:, q_cols(z)], dq_s.at[0])
            else:
                copy = remote(dq_stage.at[slot], dq_out.at[:, q_cols(z)], dq_s.at[slot],
                              dq_r.at[slot], at_ring(slot))
            copy.start()
            dq_sends.append((slot, copy))

    for x in (1, 2, 3):
        relays["part", x].wait_recv()
    kv_out = []
    for slot in (1, 7, 2, 6, 3, 5, 4, 0):
        for n, (acc, factor) in enumerate(((dk_acc, SCALE), (dv_acc, 1.0))):
            total = acc[me, slot]
            for x in range(1, NI):
                total = total + part_recv[x - 1, slot, n].astype(F32)
            if factor != 1.0:
                total = total * factor
            kv_stage[slot, n] = total.astype(BF16)
            out = (dk_out, dv_out)[n]
            if slot == 0:
                copy = pltpu.make_async_copy(kv_stage.at[0, n], out.at[:, k_cols(z)], out_s.at[n, 0])
            else:
                copy = remote(kv_stage.at[slot, n], out.at[:, k_cols(z)], out_s.at[n, slot],
                              out_r.at[n, slot], at_ring(slot))
            copy.start()
            kv_out.append((slot, n, copy))

    for copy in sends:
        copy.wait_send()
    for slot, copy in dq_sends:
        if slot == 0:
            copy.wait()
        else:
            copy.wait_send()
            came = q_cols(ring(NZ - slot))
            remote(dq_stage.at[slot], dq_out.at[:, came], dq_s.at[slot], dq_r.at[slot],
                   at_ring(slot)).wait_recv()
    for slot, n, copy in kv_out:
        if slot == 0:
            copy.wait()
        else:
            copy.wait_send()
            came = k_cols(ring(NZ - slot))
            out = (dk_out, dv_out)[n]
            remote(kv_stage.at[slot, n], out.at[:, came], out_s.at[n, slot], out_r.at[n, slot],
                   at_ring(slot)).wait_recv()


def on_device(queries, key_rows, value_rows, outputs, out_grads, log_norms):
    dma = pltpu.SemaphoreType.DMA
    width = max(len(slots) for slots in GROUPS) * GROUP * HALF
    return pl.pallas_call(
        kernel,
        out_shape=(
            jax.ShapeDtypeStruct((TOK, HQ * HD), BF16),
            jax.ShapeDtypeStruct((TOK, HK * HD), BF16),
            jax.ShapeDtypeStruct((TOK, HK * HD), BF16),
        ),
        in_specs=[pl.BlockSpec(memory_space=pl.ANY)] * 6,
        out_specs=(pl.BlockSpec(memory_space=pl.ANY),) * 3,
        scratch_shapes=[
            pltpu.VMEM((TOK, HQ * HD), BF16),
            pltpu.VMEM((TOK, HQ * HD), BF16),
            pltpu.VMEM((HQ, TOK), F32),
            pltpu.VMEM((HQ, HD), F32),
            pltpu.VMEM((NZ, 8, HD), F32),
            pltpu.VMEM((NZ, 8, HD), F32),
            pltpu.VMEM((NI, NZ, 2, TOK, HD), BF16),
            pltpu.VMEM((NZ, TOK, GCOLS), BF16),
            pltpu.VMEM((NZ, TOK, GCOLS), BF16),
            pltpu.VMEM((2, NI, HD, NZ * HALF), BF16),
            pltpu.VMEM((2, width, HD), BF16),
            pltpu.VMEM((2, width, HD), BF16),
            pltpu.VMEM((2, HD, width), F32),
            pltpu.VMEM((NZ, TOK, GCOLS), BF16),
            pltpu.VMEM((NI, NZ, TOK, HD), F32),
            pltpu.VMEM((NI, NZ, TOK, HD), F32),
            pltpu.VMEM((NI - 1, NZ, 2, TOK, HD), BF16),
            pltpu.VMEM((NI - 1, NZ, 2, TOK, HD), BF16),
            pltpu.VMEM((NZ, 2, TOK, HD), BF16),
            dma((7,)),
            dma((2, NZ)), dma((2, NZ)),
            dma((NZ,)), dma((NZ,)),
            dma((NZ,)), dma((NZ,)),
            dma((NZ,)), dma((NZ,)),
            dma((NI - 1, NZ)), dma((NI - 1, NZ)),
            dma((NZ,)), dma((NZ,)),
            dma((NI - 1,)), dma((NI - 1,)),
            dma((2, NZ)), dma((2, NZ)),
        ],
        compiler_params=pltpu.CompilerParams(
            collective_id=0, has_side_effects=True, vmem_limit_bytes=48 << 20
        ),
    )(queries, key_rows, value_rows, outputs, out_grads, log_norms)


def solution(mesh):
    rows = P(("head", "inner", "outer"), None)
    return jax.shard_map(
        on_device,
        mesh=mesh,
        in_specs=(rows,) * 5 + (P(None, ("head", "inner", "outer")),),
        out_specs=(rows,) * 3,
        check_vma=False,
    )
```

time: 905 us -> 68.3 us (0.08)
  the two profiles are of different devices: /device:TPU:1 before, /device:TPU:8 now
where the time goes in v1:
time: 68.3 us; the launch traced here: 68 us
  Pallas kernels  59.6 us (87%)
  local copies, waits for them, and re-layouts  7.75 us (11%)
    pallas_call x1, Pallas kernels, on_device(): pl.pallas_call(kernel, out_shape=(jax.ShapeDtypeStruct((TOK, HQ * HD), BF...  59.6 us
    unnamed x15, local copies, waits for them, and re-layouts  7.75 us

profile of v1, /device:TPU:8, one launch (start us, length us, event | category | flops | bytes accessed | tf_op | source)
XLA Modules:
  0.0 68.0 jit_solution(17523694265257420503)
XLA Ops:
  0.6 0.0 copy-start
  0.6 1.0 %copy-done = bf16[64,4096]{1,0:T(8,128)(2,1)S(1)} copy-done((bf16[64,4096]{1,0:T(8,128)(2,1)S(1)}, bf16[64,4096]{1,0:T(8,128)(2,1)}, u32[]{:S(2)}) %copy-start) | copy-done | bytes 524312
  1.7 0.0 copy-start.1
  1.7 1.0 %copy-done.1 = bf16[64,4096]{1,0:T(8,128)(2,1)S(1)} copy-done((bf16[64,4096]{1,0:T(8,128)(2,1)S(1)}, bf16[64,4096]{1,0:T(8,128)(2,1)}, u32[]{:S(2)}) %copy-start.1) | copy-done | bytes 524312
  2.7 0.0 copy-start.2
  2.7 1.0 %copy-done.2 = bf16[64,4096]{1,0:T(8,128)(2,1)S(1)} copy-done((bf16[64,4096]{1,0:T(8,128)(2,1)S(1)}, bf16[64,4096]{1,0:T(8,128)(2,1)}, u32[]{:S(2)}) %copy-start.2) | copy-done | bytes 524312
  3.8 0.0 copy-start.3
  3.8 0.9 %copy-done.3 = bf16[64,1024]{1,0:T(8,128)(2,1)S(1)} copy-done((bf16[64,1024]{1,0:T(8,128)(2,1)S(1)}, bf16[64,1024]{1,0:T(8,128)(2,1)}, u32[]{:S(2)}) %copy-start.3) | copy-done | bytes 131096
  4.7 0.0 copy-start.4
  4.7 0.9 %copy-done.4 = bf16[64,1024]{1,0:T(8,128)(2,1)S(1)} copy-done((bf16[64,1024]{1,0:T(8,128)(2,1)S(1)}, bf16[64,1024]{1,0:T(8,128)(2,1)}, u32[]{:S(2)}) %copy-start.4) | copy-done | bytes 131096
  5.6 0.0 copy-start.5
  5.6 0.7 %copy-done.5 = f32[32,64]{1,0:T(8,128)S(1)} copy-done((f32[32,64]{1,0:T(8,128)S(1)}, f32[32,64]{1,0:T(8,128)}, u32[]{:S(2)}) %copy-start.5) | copy-done | bytes 8216
  6.3 59.6 %shard_map.85 = (bf16[64,4096]{1,0:T(8,128)(2,1)S(1)}, bf16[64,1024]{1,0:T(8,128)(2,1)S(1)}, bf16[64,1024]{1,0:T(8,128)(2,1)S(1)}) custom-call(bf16[64,4096]{1,0:T(8,128)(2,1)S(1)} %copy-done, bf16[64,1024]{1,0:T(8,128)(2,1)S(1)} %copy-done.3, bf16[64,1024]{1,0:T(8,128)(2,1)S(1)} %copy-done.4, bf16[64,4096]{1,0:T(8,128)(2,1)S(1)} %copy-done.1, ...), custom_call_target="tpu_custom_call" | custom-call | tf_op jit(solution)/shard_map/pallas_call | solution.py:308
  65.9 0.8 %copy.12 = bf16[64,4096]{1,0:T(8,128)(2,1)} copy(bf16[64,4096]{1,0:T(8,128)(2,1)S(1)} %get-tuple-element.6) | data formatting | bytes 1048576
  66.7 0.7 copy.13
  67.3 0.7 copy.14
Async XLA Ops:
  0.6 1.0 %copy-start = (bf16[64,4096]{1,0:T(8,128)(2,1)S(1)}, bf16[64,4096]{1,0:T(8,128)(2,1)}, u32[]{:S(2)}) copy-start(bf16[64,4096]{1,0:T(8,128)(2,1)} %q_hbm.1) | copy-start | bytes 1572868
  1.7 1.0 %copy-start.1 = (bf16[64,4096]{1,0:T(8,128)(2,1)S(1)}, bf16[64,4096]{1,0:T(8,128)(2,1)}, u32[]{:S(2)}) copy-start(bf16[64,4096]{1,0:T(8,128)(2,1)} %o_hbm.1) | copy-start | bytes 1572868
  2.7 1.0 %copy-start.2 = (bf16[64,4096]{1,0:T(8,128)(2,1)S(1)}, bf16[64,4096]{1,0:T(8,128)(2,1)}, u32[]{:S(2)}) copy-start(bf16[64,4096]{1,0:T(8,128)(2,1)} %do_hbm.1) | copy-start | bytes 1572868
  3.8 0.9 %copy-start.3 = (bf16[64,1024]{1,0:T(8,128)(2,1)S(1)}, bf16[64,1024]{1,0:T(8,128)(2,1)}, u32[]{:S(2)}) copy-start(bf16[64,1024]{1,0:T(8,128)(2,1)} %k_hbm.1) | copy-start | bytes 393220
  4.7 0.9 %copy-start.4 = (bf16[64,1024]{1,0:T(8,128)(2,1)S(1)}, bf16[64,1024]{1,0:T(8,128)(2,1)}, u32[]{:S(2)}) copy-start(bf16[64,1024]{1,0:T(8,128)(2,1)} %v_hbm.1) | copy-start | bytes 393220
  5.6 0.7 %copy-start.5 = (f32[32,64]{1,0:T(8,128)S(1)}, f32[32,64]{1,0:T(8,128)}, u32[]{:S(2)}) copy-start(f32[32,64]{1,0:T(8,128)} %lse_hbm.1) | copy-start | bytes 24580

commit v2 on v1

--- a/solution.py
+++ b/solution.py
@@ -302,17 +302,29 @@
                    at_ring(slot)).wait_recv()
 
 
+def hand_on(*refs):
+    count = len(refs) // 2
+    sems = refs[-1]
+    copies = [pltpu.make_async_copy(refs[n], refs[count + n], sems.at[n]) for n in range(count)]
+    for copy in copies:
+        copy.start()
+    for copy in copies:
+        copy.wait()
+
+
 def on_device(queries, key_rows, value_rows, outputs, out_grads, log_norms):
     dma = pltpu.SemaphoreType.DMA
+    operands = (queries, key_rows, value_rows, outputs, out_grads, log_norms)
+    operands = tuple(pltpu.with_memory_space_constraint(x, pltpu.HBM) for x in operands)
     width = max(len(slots) for slots in GROUPS) * GROUP * HALF
-    return pl.pallas_call(
+    grads = pl.pallas_call(
         kernel,
         out_shape=(
             jax.ShapeDtypeStruct((TOK, HQ * HD), BF16),
             jax.ShapeDtypeStruct((TOK, HK * HD), BF16),
             jax.ShapeDtypeStruct((TOK, HK * HD), BF16),
         ),
-        in_specs=[pl.BlockSpec(memory_space=pl.ANY)] * 6,
+        in_specs=[pl.BlockSpec(memory_space=pltpu.HBM)] * 6,
         out_specs=(pl.BlockSpec(memory_space=pl.ANY),) * 3,
         scratch_shapes=[
             pltpu.VMEM((TOK, HQ * HD), BF16),
@@ -345,9 +357,17 @@
             dma((2, NZ)), dma((2, NZ)),
         ],
         compiler_params=pltpu.CompilerParams(
-            collective_id=0, has_side_effects=True, vmem_limit_bytes=48 << 20
+            collective_id=0, has_side_effects=True, vmem_limit_bytes=40 << 20
         ),
-    )(queries, key_rows, value_rows, outputs, out_grads, log_norms)
+    )(*operands)
+    grads = tuple(pltpu.with_memory_space_constraint(g, pltpu.VMEM) for g in grads)
+    return pl.pallas_call(
+        hand_on,
+        out_shape=tuple(jax.ShapeDtypeStruct(g.shape, g.dtype) for g in grads),
+        in_specs=[pl.BlockSpec(memory_space=pltpu.VMEM)] * 3,
+        out_specs=(pl.BlockSpec(memory_space=pl.ANY),) * 3,
+        scratch_shapes=[dma((3,))],
+    )(*grads)
 
 
 def solution(mesh):

time: 68.3 us -> 61.9 us (0.906)
  local copies, waits for them, and re-layouts: 7.75 us -> 0 us
  Pallas kernels: 59.6 us -> 61 us
    unnamed x15 -> x0, local copies, waits for them, and re-layouts: 7.75 us -> none
    pallas_call x0 -> x1, Pallas kernels: none -> 0.9 us  [on_device(): pl.pallas_call(hand_on, out_shape=tuple((jax.ShapeDtypeStruct(g.shape, g....]
where the time goes in v2:
time: 61.9 us; the launch traced here: 61.8 us
  Pallas kernels  61 us (99%)
  between operations  0.8 us (1%)
    pallas_call x1, Pallas kernels, on_device(): pl.pallas_call(kernel, out_shape=(jax.ShapeDtypeStruct((TOK, HQ * HD), BF...  60.1 us

profile of v2, /device:TPU:8, one launch (start us, length us, event | category | flops | bytes accessed | tf_op | source)
XLA Modules:
  0.0 61.8 jit_solution(3971984834134221890)
XLA Ops:
  0.6 60.1 %shard_map.85 = (bf16[64,4096]{1,0:T(8,128)(2,1)S(1)}, bf16[64,1024]{1,0:T(8,128)(2,1)S(1)}, bf16[64,1024]{1,0:T(8,128)(2,1)S(1)}) custom-call(bf16[64,4096]{1,0:T(8,128)(2,1)} %q_hbm.1, bf16[64,1024]{1,0:T(8,128)(2,1)} %k_hbm.1, bf16[64,1024]{1,0:T(8,128)(2,1)} %v_hbm.1, bf16[64,4096]{1,0:T(8,128)(2,1)} %o_hbm.1, bf16[64,4096]{1,0:T(8,128)(2,1)} %do_hbm.1, ...), custom_call_target="tpu_custom_call" | custom-call | tf_op jit(solution)/shard_map/pallas_call | solution.py:320
  60.7 0.9 %shard_map.86 = (bf16[64,4096]{1,0:T(8,128)(2,1)}, bf16[64,1024]{1,0:T(8,128)(2,1)}, bf16[64,1024]{1,0:T(8,128)(2,1)}) custom-call(bf16[64,4096]{1,0:T(8,128)(2,1)S(1)} %get-tuple-element.6.refs_0_, bf16[64,1024]{1,0:T(8,128)(2,1)S(1)} %get-tuple-element.7.refs_1_, bf16[64,1024]{1,0:T(8,128)(2,1)S(1)} %get-tuple-element.8.refs_2_), custom_call_target="tpu_custom_call" | custom-call | tf_op jit(solution)/shard_map/pallas_call | solution.py:364

commit v3 on v0

v3 whole, which is shorter than its diff:
```python
import jax
import jax.numpy as jnp
from jax import lax
from jax.experimental import pallas as pl
from jax.experimental.pallas import tpu as pltpu
from jax.sharding import PartitionSpec as P

HQ = 32
HK = 8
HD = 128
GROUP = HQ // HK
TOK = 64
HALF = TOK // 2
NZ = 8
NI = 4
HEADS = HK // NI
QCOLS = HEADS * GROUP * HD
KEYS = NI * HALF
ROWS = NI * GROUP * HALF
LOG2E = 1.4426950408889634
SCALE = HD ** -0.5
MESH = pl.DeviceIdType.MESH
F32 = jnp.float32
BF16 = jnp.bfloat16
UP, DOWN = 1, -1


def dot(a, b, dims):
    return lax.dot_general(a, b, (dims, ((), ())), preferred_element_type=F32)


def kernel(
    q_hbm, k_hbm, v_hbm, o_hbm, do_hbm, lse_hbm,
    dq_out, sums_out,
    o_in, do_in, lse_in, lse_wide, aux_send, aux, stats, kv, qd,
    q_rows, do_rows, dq_t, dq_stage, own, part_send, part_recv, last_stage,
    local_sem, send_sem, plane_r, ring_r, part_r, rows_r, aux_r, dq_r, last_r,
):
    me = lax.axis_index("inner")
    z = lax.axis_index("outer")

    def at_ring(step):
        return {"outer": lax.rem(z + step + NZ, NZ)}

    def at_plane(x):
        return {"inner": me ^ x}

    def q_cols(index):
        return pl.ds(pl.multiple_of(index * QCOLS, QCOLS), QCOLS)

    def k_cols(index):
        return pl.ds(pl.multiple_of(index * (HEADS * HD), HEADS * HD), HEADS * HD)

    def h_cols(index, head):
        return pl.ds(pl.multiple_of(index * (HEADS * HD) + head * HD, HD), HD)

    def remote(src, dst, send, recv, where):
        return pltpu.make_async_remote_copy(
            src_ref=src, dst_ref=dst, send_sem=send, recv_sem=recv,
            device_id=where, device_id_type=MESH,
        )

    barrier = pltpu.get_barrier_semaphore()
    for step in (UP, DOWN):
        pl.semaphore_signal(barrier, inc=1, device_id=at_ring(step), device_id_type=MESH)
    for x in range(1, NI):
        pl.semaphore_signal(barrier, inc=1, device_id=at_plane(x), device_id_type=MESH)

    mine = [
        pltpu.make_async_copy(ref.at[:, k_cols(me)], kv.at[0, 0, n], local_sem.at[0])
        for n, ref in enumerate((k_hbm, v_hbm))
    ]
    rest = [
        pltpu.make_async_copy(o_hbm, o_in, local_sem.at[1]),
        pltpu.make_async_copy(do_hbm, do_in, local_sem.at[2]),
        pltpu.make_async_copy(lse_hbm, lse_in, local_sem.at[3]),
        pltpu.make_async_copy(q_hbm.at[:, q_cols(me)], qd.at[0, 0], local_sem.at[4]),
        pltpu.make_async_copy(do_hbm.at[:, q_cols(me)], qd.at[1, 0], local_sem.at[4]),
    ]
    for copy in mine + rest:
        copy.start()
    pl.semaphore_wait(barrier, 2 + NI - 1)

    def all_of(ref, send, recv):
        return remote(ref, ref, send, recv, at_plane(1))

    PLANE, RING, QD, AUX, PART, DQ = (send_sem.at[n] for n in range(6))
    LAST = send_sem.at[6:8]

    def share(x):
        for n, ref in enumerate((k_hbm, v_hbm)):
            remote(ref.at[:, k_cols(me ^ x)], kv.at[0, x, n], PLANE, plane_r.at[x - 1],
                   at_plane(x)).start()

    def pass_first(x, n, step):
        to = -step % NZ
        src = (k_hbm, v_hbm)[n].at[:, k_cols(me)] if x == 0 else kv.at[0, x, n]
        remote(src, kv.at[to, x, n], RING, ring_r.at[to - 1, x], at_ring(step)).start()

    def pass_on(slot, x, step):
        to = (slot - step) % NZ
        remote(kv.at[slot, x], kv.at[to, x], RING, ring_r.at[to - 1, x], at_ring(step)).start()

    def arrived(slot, x):
        all_of(kv.at[slot, x], RING, ring_r.at[slot - 1, x]).wait_recv()

    share(2)
    for n in range(2):
        pass_first(0, n, UP)
        pass_first(0, n, DOWN)
    share(1)
    share(3)
    for x in (2, 3, 1):
        for n, ref in enumerate((q_hbm, do_hbm)):
            remote(ref.at[:, q_cols(me ^ x)], qd.at[n, x], QD, rows_r.at[0], at_plane(x)).start()
    for x in (1, 2, 3):
        all_of(kv.at[0, x], PLANE, plane_r.at[x - 1]).wait_recv()
        for n in range(2):
            pass_first(x, n, UP)
            pass_first(x, n, DOWN)

    def flow(up_slot, down_slot, pieces=range(NI)):
        for x in pieces:
            for slot, step, far in ((up_slot, UP, 0), (down_slot, DOWN, 1)):
                arrived(slot, x)
                if slot not in (3, 5) or x % 2 == far:
                    pass_on(slot, x, step)

    flow(7, 1)

    for copy in rest[:3]:
        copy.wait()
    lse_wide[...] = jnp.zeros_like(lse_wide)
    lse_wide[:, 0:TOK] = lse_in[...]
    norms = lse_wide[...] * LOG2E
    rows = lax.broadcasted_iota(jnp.int32, norms.shape, 0)
    lanes = lax.broadcasted_iota(jnp.int32, norms.shape, 1)
    for late in range(2):
        picked = jnp.zeros_like(norms)
        for h in range(GROUP):
            moved = norms
            shift = (h - late) * HALF % HD
            if shift:
                moved = pltpu.roll(norms, shift, 1)
            here = (rows % GROUP == h) & (lanes // HALF == h)
            picked = jnp.where(here, moved, picked)
        total = picked
        for h in range(1, GROUP):
            total = total + pltpu.roll(picked, HQ - h, 0)
        for g in range(HK):
            row = g % HEADS * 2 + late
            aux_send[g // HEADS, row:row + 1, :] = total[GROUP * g:GROUP * g + 1, :]
    ones = jnp.ones((8, HD), BF16)
    for g in range(HK):
        blocks = []
        for late in range(2):
            for h in range(GROUP):
                part = (slice(late * HALF, (late + 1) * HALF),
                        slice((g * GROUP + h) * HD, (g * GROUP + h + 1) * HD))
                blocks.append(do_in[part].astype(F32) * o_in[part].astype(F32))
        product = jnp.concatenate(blocks, axis=0)
        high = product.astype(BF16)
        low = (product - high.astype(F32)).astype(BF16)
        sums = dot(ones, high, ((1,), (1,))) + dot(ones, low, ((1,), (1,)))
        for late in range(2):
            row = 4 + g % HEADS * 2 + late
            aux_send[g // HEADS, row:row + 1, :] = sums[0:1, late * HD:(late + 1) * HD]
    aux[0] = aux_send[me]
    for x in (2, 3, 1):
        remote(aux_send.at[me ^ x], aux.at[x], AUX, aux_r.at[0], at_plane(x)).start()

    flow(6, 2)
    flow(5, 3, (0, 1))

    pltpu.make_async_copy(qd.at[:, 0], qd.at[:, 0], local_sem.at[4]).wait()
    pltpu.make_async_copy(kv.at[0, 0], kv.at[0, 0], local_sem.at[0]).wait()
    all_of(qd.at[:, 1:NI], QD, rows_r.at[0]).wait_recv()
    all_of(aux.at[1:NI], AUX, aux_r.at[0]).wait_recv()
    for x in range(NI):
        stats[:, x * HD:(x + 1) * HD] = aux[x]
        for h in range(HEADS):
            for late in range(2):
                for g in range(GROUP):
                    to = slice((x * GROUP + g) * HALF, (x * GROUP + g + 1) * HALF)
                    tok = slice(late * HALF, (late + 1) * HALF)
                    col = slice((h * GROUP + g) * HD, (h * GROUP + g + 1) * HD)
                    q_rows[h, late, to, :] = qd[0, x, tok, col]
                    do_rows[h, late, to, :] = qd[1, x, tok, col]
    dq_t[...] = jnp.zeros_like(dq_t)

    key_row = lax.broadcasted_iota(jnp.int32, (KEYS, 1), 0)
    key_device = (me ^ (key_row // HALF)) * NZ
    q_lane = lax.broadcasted_iota(jnp.int32, (1, ROWS), 1)
    q_at = ((me ^ (q_lane // (GROUP * HALF))) * NZ + z) * HALF

    def tile(h, late, keys, values, keys_t, key_at):
        q_part = q_rows[h, late]
        do_part = do_rows[h, late]
        row = h * 2 + late
        norm = stats[row:row + 1, :]
        delta = stats[row + 4:row + 5, :]
        scores = dot(keys, q_part, ((1,), (1,)))
        weights = jnp.exp2(scores * (SCALE * LOG2E) - norm)
        sign = -1 if late else 1
        allowed = key_at + key_row % HALF <= sign * q_at + q_lane % HALF
        masked = jnp.where(allowed, weights[-KEYS:], 0.0)
        weights = jnp.concatenate([weights[:-KEYS], masked], axis=0) if late else masked
        dv_add = dot(weights.astype(BF16), do_part, ((1,), (0,)))
        dweights = dot(values, do_part, ((1,), (1,)))
        dscores = (weights * (dweights - delta) * SCALE).astype(BF16)
        dk_add = dot(dscores, q_part, ((1,), (0,)))
        dq_t[h, late] += dot(keys_t, dscores, ((1,), (0,)))
        return dk_add, dv_add

    def unit(slot, h):
        key_z = lax.rem(z + slot, NZ)
        at = (key_device + key_z) * HALF
        early, late = (
            [kv[slot, :, n, part * HALF:(part + 1) * HALF, h * HD:(h + 1) * HD].reshape(KEYS, HD)
             for n in range(2)]
            for part in range(2)
        )
        keys = jnp.concatenate([early[0], late[0]], axis=0)
        values = jnp.concatenate([early[1], late[1]], axis=0)
        keys_t = keys.T
        first = tile(h, 1, keys, values, keys_t, -at)
        second = tile(h, 0, early[0], early[1], keys_t[:, 0:KEYS], at)
        for n in range(2):
            own[slot, h, n, 0:KEYS] = first[n][0:KEYS] + second[n]
            own[slot, h, n, KEYS:] = first[n][KEYS:]

    def hand_back(slot, h, first):
        step = DOWN if slot > 4 or (slot == 4 and h == 0) else UP
        to = (slot - step) % NZ
        if not first:
            all_of(part_recv.at[h, slot], PART, part_r.at[h, slot]).wait_recv()
        for n in range(2):
            total = own[slot, h, n]
            if not first:
                total = total + part_recv[h, slot, n].astype(F32)
            if to:
                part_send[h, slot, n] = total.astype(BF16)
            else:
                stage_last(max(step, 0), h, n, total)
        if to:
            remote(part_send.at[h, slot], part_recv.at[h, to], PART, part_r.at[h, to],
                   at_ring(step)).start()
        else:
            for x in (2, 3, 1, 0):
                send_last(max(step, 0), h, x, dict(at_ring(step), **at_plane(x)))

    def stage_last(way, h, n, total):
        low = total.astype(BF16)
        for x in range(NI):
            for late in range(2):
                last_stage[way, x, h, n, late * HALF:(late + 1) * HALF, :] = (
                    low[(late * NI + x) * HALF:(late * NI + x + 1) * HALF])

    def send_last(way, h, x, where):
        src, dst = last_stage.at[way, x, h], sums_out.at[way, :, :, h_cols(me, h)]
        if way == 2 and x == 0:
            pltpu.make_async_copy(src, dst, local_sem.at[6]).start()
        else:
            remote(src, dst, LAST.at[way // 2], last_r.at[way // 2], where).start()

    def finish_rows(h, late):
        back = dq_t[h, late].T.astype(BF16)
        for x in range(NI):
            for g in range(GROUP):
                dq_stage[x, late * HALF:(late + 1) * HALF,
                         (h * GROUP + g) * HD:(h * GROUP + g + 1) * HD] = (
                    back[(x * GROUP + g) * HALF:(x * GROUP + g + 1) * HALF])

    flow(5, 3, (2,))
    unit(0, 0)
    flow(5, 3, (3,))
    unit(0, 1)
    unit(7, 0)
    for slot, h in ((3, 0), (5, 1)):
        unit(slot, h)
        hand_back(slot, h, True)
    unit(1, 1)
    for h in range(HEADS):
        for n in range(2):
            stage_last(2, h, n, own[0, h, n])
        for x in (2, 3, 1, 0):
            send_last(2, h, x, at_plane(x))
    for x in range(NI):
        arrived(4, x)
    for h in range(HEADS):
        unit(4, h)
        hand_back(4, h, True)
    for slot, h in ((2, 0), (6, 1), (5, 0), (3, 1), (1, 0), (7, 1)):
        unit(slot, h)
        hand_back(slot, h, False)
    unit(6, 0)
    hand_back(6, 0, False)
    finish_rows(0, 0)
    unit(2, 1)
    hand_back(2, 1, False)
    finish_rows(0, 1)
    finish_rows(1, 0)
    finish_rows(1, 1)
    for x in (2, 3, 1):
        remote(dq_stage.at[x], dq_out.at[:, q_cols(me)], DQ, dq_r.at[0], at_plane(x)).start()
    dq_mine = pltpu.make_async_copy(dq_stage.at[0], dq_out.at[:, q_cols(me)], local_sem.at[5])
    dq_mine.start()
    for slot, h in ((7, 0), (1, 1)):
        hand_back(slot, h, False)
    all_of(kv.at[0, 1:NI], PLANE, plane_r.at[0]).wait_send()
    all_of(kv.at[1:NZ], RING, ring_r.at[0, 0]).wait_send()
    all_of(qd.at[:, 1:NI], QD, rows_r.at[0]).wait_send()
    all_of(aux.at[1:NI], AUX, aux_r.at[0]).wait_send()
    all_of(part_send.at[:, 2:NZ - 1], PART, part_r.at[0, 0]).wait_send()
    dq_mine.wait()
    all_of(dq_stage.at[1:NI], DQ, dq_r.at[0]).wait()
    pltpu.make_async_copy(last_stage.at[2, 0], last_stage.at[2, 0], local_sem.at[6]).wait()
    all_of(last_stage.at[2, 1:NI], LAST.at[1], last_r.at[1]).wait()
    all_of(last_stage.at[0:2], LAST.at[0], last_r.at[0]).wait()


def hand_on(dq_ref, sums_ref, dq_out, dk_out, dv_out, total, sems):
    copies = [pltpu.make_async_copy(dq_ref, dq_out, sems.at[0])]
    copies[0].start()
    for n, out in enumerate((dk_out, dv_out)):
        whole = sums_ref[0, n].astype(F32) + sums_ref[1, n].astype(F32) + sums_ref[2, n].astype(F32)
        total[n] = whole.astype(BF16)
        copies.append(pltpu.make_async_copy(total.at[n], out, sems.at[n + 1]))
        copies[-1].start()
    for copy in copies:
        copy.wait()


def on_device(queries, key_rows, value_rows, outputs, out_grads, log_norms):
    dma = pltpu.SemaphoreType.DMA
    operands = (queries, key_rows, value_rows, outputs, out_grads, log_norms)
    operands = tuple(pltpu.with_memory_space_constraint(x, pltpu.HBM) for x in operands)
    grads = pl.pallas_call(
        kernel,
        out_shape=(
            jax.ShapeDtypeStruct((TOK, HQ * HD), BF16),
            jax.ShapeDtypeStruct((3, 2, TOK, HK * HD), BF16),
        ),
        in_specs=[pl.BlockSpec(memory_space=pltpu.HBM)] * 6,
        out_specs=(pl.BlockSpec(memory_space=pl.ANY),) * 2,
        scratch_shapes=[
            pltpu.VMEM((TOK, HQ * HD), BF16),
            pltpu.VMEM((TOK, HQ * HD), BF16),
            pltpu.VMEM((HQ, TOK), F32),
            pltpu.VMEM((HQ, HD), F32),
            pltpu.VMEM((NI, 8, HD), F32),
            pltpu.VMEM((NI, 8, HD), F32),
            pltpu.VMEM((8, ROWS), F32),
            pltpu.VMEM((NZ, NI, 2, TOK, HEADS * HD), BF16),
            pltpu.VMEM((2, NI, TOK, QCOLS), BF16),
            pltpu.VMEM((HEADS, 2, ROWS, HD), BF16),
            pltpu.VMEM((HEADS, 2, ROWS, HD), BF16),
            pltpu.VMEM((HEADS, 2, HD, ROWS), F32),
            pltpu.VMEM((NI, TOK, QCOLS), BF16),
            pltpu.VMEM((NZ, HEADS, 2, 2 * KEYS, HD), F32),
            pltpu.VMEM((HEADS, NZ, 2, 2 * KEYS, HD), BF16),
            pltpu.VMEM((HEADS, NZ, 2, 2 * KEYS, HD), BF16),
            pltpu.VMEM((3, NI, HEADS, 2, TOK, HD), BF16),
            dma((7,)), dma((8,)),
            dma((NI - 1,)), dma((NZ - 1, NI)), dma((HEADS, NZ)),
            dma((1,)), dma((1,)), dma((1,)), dma((2,)),
        ],
        compiler_params=pltpu.CompilerParams(
            collective_id=0, has_side_effects=True, vmem_limit_bytes=40 << 20
        ),
    )(*operands)
    grads = tuple(pltpu.with_memory_space_constraint(g, pltpu.VMEM) for g in grads)
    return pl.pallas_call(
        hand_on,
        out_shape=(
            jax.ShapeDtypeStruct((TOK, HQ * HD), BF16),
            jax.ShapeDtypeStruct((TOK, HK * HD), BF16),
            jax.ShapeDtypeStruct((TOK, HK * HD), BF16),
        ),
        in_specs=[pl.BlockSpec(memory_space=pltpu.VMEM)] * 2,
        out_specs=(pl.BlockSpec(memory_space=pl.ANY),) * 3,
        scratch_shapes=[pltpu.VMEM((2, TOK, HK * HD), BF16), dma((3,))],
    )(*grads)


def solution(mesh):
    rows = P(("head", "inner", "outer"), None)
    return jax.shard_map(
        on_device,
        mesh=mesh,
        in_specs=(rows,) * 5 + (P(None, ("head", "inner", "outer")),),
        out_specs=(rows,) * 3,
        check_vma=False,
    )
```

time: 905 us -> 59.1 us (0.07); the launches traced: 894 us -> 59 us
  waiting for transfers between devices: 602 us -> 0 us
  matrix products: 98.5 us -> 0 us
  local copies, waits for them, and re-layouts: 93.6 us -> 0 us
  Pallas kernels: 0 us -> 58.4 us
  other arithmetic: 45.2 us -> 0 us
  starting transfers between devices: 41.6 us -> 0 us
  blocking collectives: 9.43 us -> 0 us
    ppermute x64 -> x0, waiting for transfers between devices: 547 us -> none  [shifted(): return lax.ppermute(block, axis, route)]
    dot_general x160 -> x0, matrix products: 98.5 us -> none  [the longest x32 39.8 us: tile_grads(): jnp.einsum('skgtu,sukd->stkgd', dscores, k_heads, preferred_element_type=...]
    pallas_call x0 -> x2, Pallas kernels: none -> 58.4 us  [the longest x1 57.5 us: on_device(): pl.pallas_call(kernel, out_shape=(jax.ShapeDtypeStruct((TOK, HQ * HD), BF...]
    all_to_all x8 -> x0, waiting for transfers between devices: 54.9 us -> none  [the longest x1 8.16 us: on_device(): lax.all_to_all(queries, 'head', split_axis=1, concat_axis=0, tiled=True)]
    add x64 -> x0, other arithmetic: 36.3 us -> none  [the longest x32 27.5 us: cycle_step(): grad_next = shifted(grad_cur + grad_add, ('inner', 'outer'), 1)]
    all_to_all x8 -> x0, starting transfers between devices: 32 us -> none  [the longest x1 7.61 us: on_device(): lax.all_to_all(log_norms, 'head', split_axis=0, concat_axis=1, tiled=True)]
    while x224 -> x0, local copies, waits for them, and re-layouts: 30.9 us -> none
    reshape x128 -> x0, local copies, waits for them, and re-layouts: 27.9 us -> none  [the longest x64 25.1 us: tile_grads(): delta_part.reshape(kv_heads, group_size, seq_count, q_count)]
  transfers between devices with their start and end apart: 72 -> 0, of which waited for: 40 -> 0; matrix products, arithmetic and copies ran while one was open for 9% -> 0% of each run, Pallas kernels for 0% -> 0%
where the time goes in v3:
time: 59.1 us; the launch traced here: 59 us
  Pallas kernels  58.4 us (99%)
  between operations  0.64 us (1%)
    pallas_call x1, Pallas kernels, on_device(): pl.pallas_call(kernel, out_shape=(jax.ShapeDtypeStruct((TOK, HQ * HD), BF...  57.5 us

profile of v3, /device:TPU:1, one launch (start us, length us, event | category | flops | bytes accessed | tf_op | source)
XLA Modules:
  0.0 59.0 jit_solution(14088450459209798480)
XLA Ops:
  0.6 57.5 %shard_map.85 = (bf16[64,4096]{1,0:T(8,128)(2,1)S(1)}, bf16[3,2,64,1024]{3,2,1,0:T(8,128)(2,1)S(1)}) custom-call(bf16[64,4096]{1,0:T(8,128)(2,1)} %q_hbm.1, bf16[64,1024]{1,0:T(8,128)(2,1)} %k_hbm.1, bf16[64,1024]{1,0:T(8,128)(2,1)} %v_hbm.1, bf16[64,4096]{1,0:T(8,128)(2,1)} %o_hbm.1, bf16[64,4096]{1,0:T(8,128)(2,1)} %do_hbm.1, f32[32,64]{1,0:T(8,128)} %lse_hbm.1), custom_call_target="tpu_custom_call" | custom-call | tf_op jit(solution)/shard_map/pallas_call | solution.py:338
  58.1 0.9 %shard_map.86 = (bf16[64,4096]{1,0:T(8,128)(2,1)}, bf16[64,1024]{1,0:T(8,128)(2,1)}, bf16[64,1024]{1,0:T(8,128)(2,1)}) custom-call(bf16[64,4096]{1,0:T(8,128)(2,1)S(1)} %get-tuple-element.5.dq_ref, bf16[3,2,64,1024]{3,2,1,0:T(8,128)(2,1)S(1)} %get-tuple-element.6.sums_ref), custom_call_target="tpu_custom_call" | custom-call | tf_op jit(solution)/shard_map/pallas_call | solution.py:373

commit v4 on v3

--- a/solution.py
+++ b/solution.py
@@ -110,9 +110,9 @@
         pass_first(0, n, DOWN)
     share(1)
     share(3)
-    for x in (2, 3, 1):
+    for x in (1, 2, 3):
         for n, ref in enumerate((q_hbm, do_hbm)):
-            remote(ref.at[:, q_cols(me ^ x)], qd.at[n, x], QD, rows_r.at[0], at_plane(x)).start()
+            remote(ref.at[:, q_cols(me ^ x)], qd.at[n, x], QD, rows_r.at[x // 2], at_plane(x)).start()
     for x in (1, 2, 3):
         all_of(kv.at[0, x], PLANE, plane_r.at[x - 1]).wait_recv()
         for n in range(2):
@@ -167,25 +167,26 @@
             aux_send[g // HEADS, row:row + 1, :] = sums[0:1, late * HD:(late + 1) * HD]
     aux[0] = aux_send[me]
     for x in (2, 3, 1):
-        remote(aux_send.at[me ^ x], aux.at[x], AUX, aux_r.at[0], at_plane(x)).start()
-
-    flow(6, 2)
-    flow(5, 3, (0, 1))
-
-    pltpu.make_async_copy(qd.at[:, 0], qd.at[:, 0], local_sem.at[4]).wait()
-    pltpu.make_async_copy(kv.at[0, 0], kv.at[0, 0], local_sem.at[0]).wait()
-    all_of(qd.at[:, 1:NI], QD, rows_r.at[0]).wait_recv()
-    all_of(aux.at[1:NI], AUX, aux_r.at[0]).wait_recv()
-    for x in range(NI):
-        stats[:, x * HD:(x + 1) * HD] = aux[x]
-        for h in range(HEADS):
-            for late in range(2):
-                for g in range(GROUP):
-                    to = slice((x * GROUP + g) * HALF, (x * GROUP + g + 1) * HALF)
-                    tok = slice(late * HALF, (late + 1) * HALF)
-                    col = slice((h * GROUP + g) * HD, (h * GROUP + g + 1) * HD)
-                    q_rows[h, late, to, :] = qd[0, x, tok, col]
-                    do_rows[h, late, to, :] = qd[1, x, tok, col]
+        remote(aux_send.at[me ^ x], aux.at[x], AUX, aux_r.at[x // 2], at_plane(x)).start()
+
+    def rows_of(first):
+        if first == 0:
+            pltpu.make_async_copy(qd.at[:, 0], qd.at[:, 0], local_sem.at[4]).wait()
+            pltpu.make_async_copy(kv.at[0, 0], kv.at[0, 0], local_sem.at[0]).wait()
+        came = slice(max(first, 1), first + 2)
+        all_of(qd.at[:, came], QD, rows_r.at[first // 2]).wait_recv()
+        all_of(aux.at[came], AUX, aux_r.at[first // 2]).wait_recv()
+        for x in range(first, first + 2):
+            stats[:, x * HD:(x + 1) * HD] = aux[x]
+            for h in range(HEADS):
+                for late in range(2):
+                    for g in range(GROUP):
+                        to = slice((x * GROUP + g) * HALF, (x * GROUP + g + 1) * HALF)
+                        tok = slice(late * HALF, (late + 1) * HALF)
+                        col = slice((h * GROUP + g) * HD, (h * GROUP + g + 1) * HD)
+                        q_rows[h, late, to, :] = qd[0, x, tok, col]
+                        do_rows[h, late, to, :] = qd[1, x, tok, col]
+
     dq_t[...] = jnp.zeros_like(dq_t)
 
     key_row = lax.broadcasted_iota(jnp.int32, (KEYS, 1), 0)
@@ -193,26 +194,27 @@
     q_lane = lax.broadcasted_iota(jnp.int32, (1, ROWS), 1)
     q_at = ((me ^ (q_lane // (GROUP * HALF))) * NZ + z) * HALF
 
-    def tile(h, late, keys, values, keys_t, key_at):
-        q_part = q_rows[h, late]
-        do_part = do_rows[h, late]
+    def tile(h, late, keys, values, keys_t, key_at, span):
+        q_part = q_rows[h, late, span]
+        do_part = do_rows[h, late, span]
         row = h * 2 + late
-        norm = stats[row:row + 1, :]
-        delta = stats[row + 4:row + 5, :]
+        norm = stats[row:row + 1, span]
+        delta = stats[row + 4:row + 5, span]
         scores = dot(keys, q_part, ((1,), (1,)))
         weights = jnp.exp2(scores * (SCALE * LOG2E) - norm)
         sign = -1 if late else 1
-        allowed = key_at + key_row % HALF <= sign * q_at + q_lane % HALF
+        allowed = key_at + key_row % HALF <= (sign * q_at + q_lane % HALF)[:, span]
         masked = jnp.where(allowed, weights[-KEYS:], 0.0)
         weights = jnp.concatenate([weights[:-KEYS], masked], axis=0) if late else masked
         dv_add = dot(weights.astype(BF16), do_part, ((1,), (0,)))
         dweights = dot(values, do_part, ((1,), (1,)))
         dscores = (weights * (dweights - delta) * SCALE).astype(BF16)
         dk_add = dot(dscores, q_part, ((1,), (0,)))
-        dq_t[h, late] += dot(keys_t, dscores, ((1,), (0,)))
+        dq_t[h, late, :, span] += dot(keys_t, dscores, ((1,), (0,)))
         return dk_add, dv_add
 
-    def unit(slot, h):
+    def unit(slot, h, part=None):
+        span = slice(0, ROWS) if part is None else slice(part * ROWS // 2, (part + 1) * ROWS // 2)
         key_z = lax.rem(z + slot, NZ)
         at = (key_device + key_z) * HALF
         early, late = (
@@ -223,11 +225,15 @@
         keys = jnp.concatenate([early[0], late[0]], axis=0)
         values = jnp.concatenate([early[1], late[1]], axis=0)
         keys_t = keys.T
-        first = tile(h, 1, keys, values, keys_t, -at)
-        second = tile(h, 0, early[0], early[1], keys_t[:, 0:KEYS], at)
+        first = tile(h, 1, keys, values, keys_t, -at, span)
+        second = tile(h, 0, early[0], early[1], keys_t[:, 0:KEYS], at, span)
         for n in range(2):
-            own[slot, h, n, 0:KEYS] = first[n][0:KEYS] + second[n]
-            own[slot, h, n, KEYS:] = first[n][KEYS:]
+            if part == 1:
+                own[slot, h, n, 0:KEYS] += first[n][0:KEYS] + second[n]
+                own[slot, h, n, KEYS:] += first[n][KEYS:]
+            else:
+                own[slot, h, n, 0:KEYS] = first[n][0:KEYS] + second[n]
+                own[slot, h, n, KEYS:] = first[n][KEYS:]
 
     def hand_back(slot, h, first):
         step = DOWN if slot > 4 or (slot == 4 and h == 0) else UP
@@ -263,23 +269,39 @@
         else:
             remote(src, dst, LAST.at[way // 2], last_r.at[way // 2], where).start()
 
-    def finish_rows(h, late):
-        back = dq_t[h, late].T.astype(BF16)
-        for x in range(NI):
-            for g in range(GROUP):
-                dq_stage[x, late * HALF:(late + 1) * HALF,
-                         (h * GROUP + g) * HD:(h * GROUP + g + 1) * HD] = (
-                    back[(x * GROUP + g) * HALF:(x * GROUP + g + 1) * HALF])
-
+    def finish_rows(h):
+        for late in range(2):
+            back = dq_t[h, late].T.astype(BF16)
+            for x in range(NI):
+                for g in range(GROUP):
+                    dq_stage[h, x, late * HALF:(late + 1) * HALF, g * HD:(g + 1) * HD] = (
+                        back[(x * GROUP + g) * HALF:(x * GROUP + g + 1) * HALF])
+        cols = pl.ds(pl.multiple_of((me * HEADS + h) * GROUP * HD, GROUP * HD), GROUP * HD)
+        for x in (2, 3, 1):
+            remote(dq_stage.at[h, x], dq_out.at[:, cols], DQ, dq_r.at[0], at_plane(x)).start()
+        pltpu.make_async_copy(dq_stage.at[h, 0], dq_out.at[:, cols], local_sem.at[5]).start()
+
+    rows_of(0)
+    for x, units in enumerate((((0, 0),), ((0, 1),), ((7, 0),), ((1, 1),))):
+        flow(6, 2, (x,))
+        for slot, h in units:
+            unit(slot, h, 0)
+    unit(7, 1, 0)
+    unit(1, 0, 0)
+    for x, units in enumerate((((6, 0), (2, 1)), ((6, 1), (2, 0)))):
+        flow(5, 3, (x,))
+        for slot, h in units:
+            unit(slot, h, 0)
+    rows_of(2)
     flow(5, 3, (2,))
-    unit(0, 0)
+    unit(0, 0, 1)
     flow(5, 3, (3,))
-    unit(0, 1)
-    unit(7, 0)
+    unit(0, 1, 1)
     for slot, h in ((3, 0), (5, 1)):
         unit(slot, h)
         hand_back(slot, h, True)
-    unit(1, 1)
+    for slot, h in ((7, 0), (1, 1)):
+        unit(slot, h, 1)
     for h in range(HEADS):
         for n in range(2):
             stage_last(2, h, n, own[0, h, n])
@@ -290,30 +312,33 @@
     for h in range(HEADS):
         unit(4, h)
         hand_back(4, h, True)
-    for slot, h in ((2, 0), (6, 1), (5, 0), (3, 1), (1, 0), (7, 1)):
-        unit(slot, h)
+    for slot, h in ((2, 0), (6, 1)):
+        unit(slot, h, 1)
         hand_back(slot, h, False)
-    unit(6, 0)
+    unit(5, 0)
+    unit(3, 1)
+    hand_back(5, 0, False)
+    hand_back(3, 1, False)
+    unit(1, 0, 1)
+    unit(6, 0, 1)
+    hand_back(1, 0, False)
+    finish_rows(0)
+    unit(7, 1, 1)
+    hand_back(7, 1, False)
     hand_back(6, 0, False)
-    finish_rows(0, 0)
-    unit(2, 1)
+    unit(2, 1, 1)
     hand_back(2, 1, False)
-    finish_rows(0, 1)
-    finish_rows(1, 0)
-    finish_rows(1, 1)
-    for x in (2, 3, 1):
-        remote(dq_stage.at[x], dq_out.at[:, q_cols(me)], DQ, dq_r.at[0], at_plane(x)).start()
-    dq_mine = pltpu.make_async_copy(dq_stage.at[0], dq_out.at[:, q_cols(me)], local_sem.at[5])
-    dq_mine.start()
+    finish_rows(1)
     for slot, h in ((7, 0), (1, 1)):
         hand_back(slot, h, False)
+
     all_of(kv.at[0, 1:NI], PLANE, plane_r.at[0]).wait_send()
     all_of(kv.at[1:NZ], RING, ring_r.at[0, 0]).wait_send()
     all_of(qd.at[:, 1:NI], QD, rows_r.at[0]).wait_send()
     all_of(aux.at[1:NI], AUX, aux_r.at[0]).wait_send()
     all_of(part_send.at[:, 2:NZ - 1], PART, part_r.at[0, 0]).wait_send()
-    dq_mine.wait()
-    all_of(dq_stage.at[1:NI], DQ, dq_r.at[0]).wait()
+    pltpu.make_async_copy(dq_stage.at[:, 0], dq_stage.at[:, 0], local_sem.at[5]).wait()
+    all_of(dq_stage.at[:, 1:NI], DQ, dq_r.at[0]).wait()
     pltpu.make_async_copy(last_stage.at[2, 0], last_stage.at[2, 0], local_sem.at[6]).wait()
     all_of(last_stage.at[2, 1:NI], LAST.at[1], last_r.at[1]).wait()
     all_of(last_stage.at[0:2], LAST.at[0], last_r.at[0]).wait()
@@ -356,14 +381,14 @@
             pltpu.VMEM((HEADS, 2, ROWS, HD), BF16),
             pltpu.VMEM((HEADS, 2, ROWS, HD), BF16),
             pltpu.VMEM((HEADS, 2, HD, ROWS), F32),
-            pltpu.VMEM((NI, TOK, QCOLS), BF16),
+            pltpu.VMEM((HEADS, NI, TOK, GROUP * HD), BF16),
             pltpu.VMEM((NZ, HEADS, 2, 2 * KEYS, HD), F32),
             pltpu.VMEM((HEADS, NZ, 2, 2 * KEYS, HD), BF16),
             pltpu.VMEM((HEADS, NZ, 2, 2 * KEYS, HD), BF16),
             pltpu.VMEM((3, NI, HEADS, 2, TOK, HD), BF16),
             dma((7,)), dma((8,)),
             dma((NI - 1,)), dma((NZ - 1, NI)), dma((HEADS, NZ)),
-            dma((1,)), dma((1,)), dma((1,)), dma((2,)),
+            dma((2,)), dma((2,)), dma((1,)), dma((2,)),
         ],
         compiler_params=pltpu.CompilerParams(
             collective_id=0, has_side_effects=True, vmem_limit_bytes=40 << 20

time: 59.1 us -> 56.8 us (0.961)
  Pallas kernels: 58.4 us -> 55.9 us
    pallas_call x1, Pallas kernels: 57.5 us -> 55 us  [on_device(): pl.pallas_call(kernel, out_shape=(jax.ShapeDtypeStruct((TOK, HQ * HD), BF...]
where the time goes in v4:
time: 56.8 us; the launch traced here: 56.7 us
  Pallas kernels  55.9 us (98%)
  between operations  0.8 us (1%)
    pallas_call x1, Pallas kernels, on_device(): pl.pallas_call(kernel, out_shape=(jax.ShapeDtypeStruct((TOK, HQ * HD), BF...  55 us

profile of v4, /device:TPU:1, one launch (start us, length us, event | category | flops | bytes accessed | tf_op | source)
XLA Modules:
  0.0 56.7 jit_solution(1335445785604411490)
XLA Ops:
  0.6 55.0 %shard_map.85 = (bf16[64,4096]{1,0:T(8,128)(2,1)S(1)}, bf16[3,2,64,1024]{3,2,1,0:T(8,128)(2,1)S(1)}) custom-call(bf16[64,4096]{1,0:T(8,128)(2,1)} %q_hbm.1, bf16[64,1024]{1,0:T(8,128)(2,1)} %k_hbm.1, bf16[64,1024]{1,0:T(8,128)(2,1)} %v_hbm.1, bf16[64,4096]{1,0:T(8,128)(2,1)} %o_hbm.1, bf16[64,4096]{1,0:T(8,128)(2,1)} %do_hbm.1, f32[32,64]{1,0:T(8,128)} %lse_hbm.1), custom_call_target="tpu_custom_call" | custom-call | tf_op jit(solution)/shard_map/pallas_call | solution.py:363
  55.7 0.9 %shard_map.86 = (bf16[64,4096]{1,0:T(8,128)(2,1)}, bf16[64,1024]{1,0:T(8,128)(2,1)}, bf16[64,1024]{1,0:T(8,128)(2,1)}) custom-call(bf16[64,4096]{1,0:T(8,128)(2,1)S(1)} %get-tuple-element.5.dq_ref, bf16[3,2,64,1024]{3,2,1,0:T(8,128)(2,1)S(1)} %get-tuple-element.6.sums_ref), custom_call_target="tpu_custom_call" | custom-call | tf_op jit(solution)/shard_map/pallas_call | solution.py:398

commit v5 on v4

--- a/solution.py
+++ b/solution.py
@@ -77,8 +77,6 @@
         pltpu.make_async_copy(q_hbm.at[:, q_cols(me)], qd.at[0, 0], local_sem.at[4]),
         pltpu.make_async_copy(do_hbm.at[:, q_cols(me)], qd.at[1, 0], local_sem.at[4]),
     ]
-    for copy in mine + rest:
-        copy.start()
     pl.semaphore_wait(barrier, 2 + NI - 1)
 
     def all_of(ref, send, recv):
@@ -110,6 +108,8 @@
         pass_first(0, n, DOWN)
     share(1)
     share(3)
+    for copy in mine + rest:
+        copy.start()
     for x in (1, 2, 3):
         for n, ref in enumerate((q_hbm, do_hbm)):
             remote(ref.at[:, q_cols(me ^ x)], qd.at[n, x], QD, rows_r.at[x // 2], at_plane(x)).start()
@@ -197,21 +197,25 @@
     def tile(h, late, keys, values, keys_t, key_at, span):
         q_part = q_rows[h, late, span]
         do_part = do_rows[h, late, span]
-        row = h * 2 + late
-        norm = stats[row:row + 1, span]
-        delta = stats[row + 4:row + 5, span]
         scores = dot(keys, q_part, ((1,), (1,)))
-        weights = jnp.exp2(scores * (SCALE * LOG2E) - norm)
-        sign = -1 if late else 1
-        allowed = key_at + key_row % HALF <= (sign * q_at + q_lane % HALF)[:, span]
-        masked = jnp.where(allowed, weights[-KEYS:], 0.0)
-        weights = jnp.concatenate([weights[:-KEYS], masked], axis=0) if late else masked
-        dv_add = dot(weights.astype(BF16), do_part, ((1,), (0,)))
         dweights = dot(values, do_part, ((1,), (1,)))
-        dscores = (weights * (dweights - delta) * SCALE).astype(BF16)
-        dk_add = dot(dscores, q_part, ((1,), (0,)))
-        dq_t[h, late, :, span] += dot(keys_t, dscores, ((1,), (0,)))
-        return dk_add, dv_add
+
+        def finish():
+            row = h * 2 + late
+            norm = stats[row:row + 1, span]
+            delta = stats[row + 4:row + 5, span]
+            weights = jnp.exp2(scores * (SCALE * LOG2E) - norm)
+            sign = -1 if late else 1
+            allowed = key_at + key_row % HALF <= (sign * q_at + q_lane % HALF)[:, span]
+            masked = jnp.where(allowed, weights[-KEYS:], 0.0)
+            full = jnp.concatenate([weights[:-KEYS], masked], axis=0) if late else masked
+            dscores = (full * (dweights - delta) * SCALE).astype(BF16)
+            dv_add = dot(full.astype(BF16), do_part, ((1,), (0,)))
+            dk_add = dot(dscores, q_part, ((1,), (0,)))
+            dq_t[h, late, :, span] += dot(keys_t, dscores, ((1,), (0,)))
+            return dk_add, dv_add
+
+        return finish
 
     def unit(slot, h, part=None):
         span = slice(0, ROWS) if part is None else slice(part * ROWS // 2, (part + 1) * ROWS // 2)
@@ -227,6 +231,7 @@
         keys_t = keys.T
         first = tile(h, 1, keys, values, keys_t, -at, span)
         second = tile(h, 0, early[0], early[1], keys_t[:, 0:KEYS], at, span)
+        first, second = first(), second()
         for n in range(2):
             if part == 1:
                 own[slot, h, n, 0:KEYS] += first[n][0:KEYS] + second[n]
@@ -296,17 +301,10 @@
     flow(5, 3, (2,))
     unit(0, 0, 1)
     flow(5, 3, (3,))
-    unit(0, 1, 1)
     for slot, h in ((3, 0), (5, 1)):
         unit(slot, h)
         hand_back(slot, h, True)
-    for slot, h in ((7, 0), (1, 1)):
-        unit(slot, h, 1)
-    for h in range(HEADS):
-        for n in range(2):
-            stage_last(2, h, n, own[0, h, n])
-        for x in (2, 3, 1, 0):
-            send_last(2, h, x, at_plane(x))
+    unit(0, 1, 1)
     for x in range(NI):
         arrived(4, x)
     for h in range(HEADS):
@@ -319,6 +317,12 @@
     unit(3, 1)
     hand_back(5, 0, False)
     hand_back(3, 1, False)
+    for h in range(HEADS):
+        for n in range(2):
+            stage_last(2, h, n, own[0, h, n])
+        for x in (2, 3, 1, 0):
+            send_last(2, h, x, at_plane(x))
+    unit(7, 0, 1)
     unit(1, 0, 1)
     unit(6, 0, 1)
     hand_back(1, 0, False)
@@ -326,6 +330,7 @@
     unit(7, 1, 1)
     hand_back(7, 1, False)
     hand_back(6, 0, False)
+    unit(1, 1, 1)
     unit(2, 1, 1)
     hand_back(2, 1, False)
     finish_rows(1)

time: 56.8 us -> 56.2 us (0.989)
  no operation moved by 1% of the time
where the time goes in v5:
time: 56.2 us
  Pallas kernels  55.5 us (99%)
  between operations  0.64 us (1%)
    pallas_call x1, Pallas kernels, on_device(): pl.pallas_call(kernel, out_shape=(jax.ShapeDtypeStruct((TOK, HQ * HD), BF...  54.6 us

profile of v5, /device:TPU:1, one launch (start us, length us, event | category | flops | bytes accessed | tf_op | source)
XLA Modules:
  0.0 56.2 jit_solution(5315313131646089596)
XLA Ops:
  0.6 54.6 %shard_map.85 = (bf16[64,4096]{1,0:T(8,128)(2,1)S(1)}, bf16[3,2,64,1024]{3,2,1,0:T(8,128)(2,1)S(1)}) custom-call(bf16[64,4096]{1,0:T(8,128)(2,1)} %q_hbm.1, bf16[64,1024]{1,0:T(8,128)(2,1)} %k_hbm.1, bf16[64,1024]{1,0:T(8,128)(2,1)} %v_hbm.1, bf16[64,4096]{1,0:T(8,128)(2,1)} %o_hbm.1, bf16[64,4096]{1,0:T(8,128)(2,1)} %do_hbm.1, f32[32,64]{1,0:T(8,128)} %lse_hbm.1), custom_call_target="tpu_custom_call" | custom-call | tf_op jit(solution)/shard_map/pallas_call | solution.py:368
  55.3 0.9 %shard_map.86 = (bf16[64,4096]{1,0:T(8,128)(2,1)}, bf16[64,1024]{1,0:T(8,128)(2,1)}, bf16[64,1024]{1,0:T(8,128)(2,1)}) custom-call(bf16[64,4096]{1,0:T(8,128)(2,1)S(1)} %get-tuple-element.5.dq_ref, bf16[3,2,64,1024]{3,2,1,0:T(8,128)(2,1)S(1)} %get-tuple-element.6.sums_ref), custom_call_target="tpu_custom_call" | custom-call | tf_op jit(solution)/shard_map/pallas_call | solution.py:403

commit v6 on v5

--- a/solution.py
+++ b/solution.py
@@ -115,9 +115,8 @@
             remote(ref.at[:, q_cols(me ^ x)], qd.at[n, x], QD, rows_r.at[x // 2], at_plane(x)).start()
     for x in (1, 2, 3):
         all_of(kv.at[0, x], PLANE, plane_r.at[x - 1]).wait_recv()
-        for n in range(2):
-            pass_first(x, n, UP)
-            pass_first(x, n, DOWN)
+        pass_on(0, x, UP)
+        pass_on(0, x, DOWN)
 
     def flow(up_slot, down_slot, pieces=range(NI)):
         for x in pieces:

time: 56.2 us -> 56.2 us (level)
  no operation moved by 1% of the time
where the time goes in v6:
time: 56.2 us
  Pallas kernels  55.5 us (99%)
  between operations  0.64 us (1%)
    pallas_call x1, Pallas kernels, on_device(): pl.pallas_call(kernel, out_shape=(jax.ShapeDtypeStruct((TOK, HQ * HD), BF...  54.6 us

profile of v6, /device:TPU:1, one launch (start us, length us, event | category | flops | bytes accessed | tf_op | source)
XLA Modules:
  0.0 56.2 jit_solution(496041301507638647)
XLA Ops:
  0.6 54.6 %shard_map.85 = (bf16[64,4096]{1,0:T(8,128)(2,1)S(1)}, bf16[3,2,64,1024]{3,2,1,0:T(8,128)(2,1)S(1)}) custom-call(bf16[64,4096]{1,0:T(8,128)(2,1)} %q_hbm.1, bf16[64,1024]{1,0:T(8,128)(2,1)} %k_hbm.1, bf16[64,1024]{1,0:T(8,128)(2,1)} %v_hbm.1, bf16[64,4096]{1,0:T(8,128)(2,1)} %o_hbm.1, bf16[64,4096]{1,0:T(8,128)(2,1)} %do_hbm.1, f32[32,64]{1,0:T(8,128)} %lse_hbm.1), custom_call_target="tpu_custom_call" | custom-call | tf_op jit(solution)/shard_map/pallas_call | solution.py:367
  55.3 0.9 %shard_map.86 = (bf16[64,4096]{1,0:T(8,128)(2,1)}, bf16[64,1024]{1,0:T(8,128)(2,1)}, bf16[64,1024]{1,0:T(8,128)(2,1)}) custom-call(bf16[64,4096]{1,0:T(8,128)(2,1)S(1)} %get-tuple-element.5.dq_ref, bf16[3,2,64,1024]{3,2,1,0:T(8,128)(2,1)S(1)} %get-tuple-element.6.sums_ref), custom_call_target="tpu_custom_call" | custom-call | tf_op jit(solution)/shard_map/pallas_call | solution.py:402
